TPU v7x, 256 devices: a whole 4x4x8 slice. The times are simulated.
256 devices in a mesh: seq: 16 (over z_lo, x, core), head: 16 (over z_hi, y).
Axes of the slice: x: 4, y: 4, z: 8 (z_hi: 4, z_lo: 2; z = z_hi * 2 + z_lo), core: 2. Of those that a mesh axis runs over, the one named last changes fastest.
Arguments:
- queries: bfloat16 [32768, 4096], P(('seq', 'head')), may hold values from -6 to 6
- outputs: bfloat16 [32768, 4096], P(('seq', 'head')), may hold values from -6 to 6
- out_grads: bfloat16 [32768, 4096], P(('seq', 'head')), may hold values from -0.5 to 0.5
- log_norms: bfloat16 [32768, 32], P(('seq', 'head')), may hold values from 2 to 5
- keys: bfloat16 [32768, 512], P(('seq', 'head')), may hold values from -6 to 6
- values: bfloat16 [32768, 512], P(('seq', 'head')), may hold values from -6 to 6
- doc_start: int32 [256], P('seq'), may hold values from 0 to 255, as said below
Outputs:
- query_grads: bfloat16 [32768, 4096], P(('seq', 'head'))
- key_grads: bfloat16 [32768, 512], P(('seq', 'head'))
- value_grads: bfloat16 [32768, 512], P(('seq', 'head'))
Inputs may be any that keep to these rules, and one draw needn't show every extreme that they name: doc_start never falls, doc_start[b] <= b, and equals b exactly where a document begins; every document covers 1 to 8 blocks, one document of exactly 8 blocks has 7 of its blocks before block 16 and one at it, and the last block begins a document.
All inputs are finite; a program needn't handle non-finite values.
Results may differ from a plain program's by a relative error of at most 0.0053.
Values may be sent and summed in bfloat16 or wider, within the bound.
No kernel may reach another device: no remote copies, remote signals or barrier semaphores. Data moves between devices by JAX's collectives and lax.ppermute only.
A program may use at most 128 MiB of HBM per device.

v0:
```python
import functools

import jax
import jax.numpy as jnp
from jax import lax
from jax.experimental import pallas as pl
from jax.experimental.pallas import tpu as pltpu
from jax.sharding import PartitionSpec as P

H = 32
KVH = 4
DH = 128
BLOCK = 128
GQ = 8
ROW = 4
WIDE = GQ * DH
SCALE = DH ** (-0.5)
AXES = ("seq", "head")
PAIR = 2 * DH
HALF = GQ // 2 * BLOCK
STAT = 2 * HALF
PIECE = STAT + 16
HEAVY = 20_000_000_000
F32 = jnp.float32
BF16 = jnp.bfloat16

VMEM = pl.BlockSpec(memory_space=pltpu.VMEM)
HBM = pl.BlockSpec(memory_space=pltpu.HBM)
SMEM = pl.BlockSpec(memory_space=pltpu.SMEM)


def nt(left, right):
    return lax.dot_general(left, right, (((1,), (1,)), ((), ())), preferred_element_type=F32)


def nn(left, right):
    return jnp.dot(left, right, preferred_element_type=F32)


def pack_kv(keys, values, piece0, piece1, piece2, piece3, sems):
    place = lax.rem(lax.axis_index("head"), ROW)
    copies = []
    for shift, piece in enumerate((piece0, piece1, piece2, piece3)):
        columns = pl.ds(pl.multiple_of(lax.rem(place + shift, ROW) * DH, DH), DH)
        for part, source in enumerate((keys, values)):
            copies.append(
                pltpu.make_async_copy(
                    source.at[:, columns],
                    piece.at[:, pl.ds(part * DH, DH)],
                    sems.at[shift, part],
                )
            )
    for copy in copies:
        copy.start()
    for copy in copies:
        copy.wait()


def pack(shifts, queries, outputs, grads, norms, *rest):
    place = lax.rem(lax.axis_index("head"), ROW)
    count = len(shifts)
    pieces = rest[:count]
    held, held_norms, sems = rest[count:]
    loads = []
    for slot, shift in enumerate(shifts):
        group = lax.rem(place + shift, ROW)
        span = pl.ds(pl.multiple_of(group * WIDE, WIDE), WIDE)
        loads.append(
            [
                pltpu.make_async_copy(
                    source.at[:, span], held.at[slot, part], sems.at[slot, part]
                )
                for part, source in enumerate((grads, outputs, queries))
            ]
        )
    norm_copy = pltpu.make_async_copy(norms, held_norms, sems.at[0, 3])
    norm_copy.start()
    for load in loads:
        for copy in load:
            copy.start()
    norm_copy.wait()
    turned = held_norms[...].astype(F32)
    ones = jnp.ones((16, DH), BF16)
    row_id = lax.broadcasted_iota(jnp.int32, (16, BLOCK), 0)
    kind = row_id // 4
    head_id = lax.broadcasted_iota(jnp.int32, (H, BLOCK), 0)
    for slot, (shift, piece) in enumerate(zip(shifts, pieces)):
        group = lax.rem(place + shift, ROW)
        loads[slot][0].wait()
        loads[slot][1].wait()
        stats = [jnp.zeros((16, BLOCK), F32)] * 2
        for head in range(GQ):
            cut = slice(head * DH, (head + 1) * DH)
            grad = held[slot, 0, :, cut]
            product = grad.astype(F32) * held[slot, 1, :, cut].astype(F32)
            high = product.astype(BF16)
            low = (product - high.astype(F32)).astype(BF16)
            dots = nt(ones, high) + nt(ones, low)
            first = dots.astype(BF16).astype(F32)
            second = (dots - first).astype(BF16).astype(F32)
            third = dots - first - second
            norm = jnp.sum(
                jnp.where(head_id == group * GQ + head, turned, 0.0), axis=0, keepdims=True
            )
            both = jnp.where(
                kind == 0,
                norm,
                jnp.where(kind == 1, first, jnp.where(kind == 2, second, third)),
            )
            stats[head % 2] = jnp.where(row_id % 4 == head // 2, both, stats[head % 2])
            rows = slice(HALF + head // 2 * BLOCK, HALF + (head // 2 + 1) * BLOCK)
            piece[rows, head % 2 * DH : (head % 2 + 1) * DH] = grad
        piece[STAT:, :DH] = stats[0].astype(BF16)
        piece[STAT:, DH:] = stats[1].astype(BF16)
    for slot, piece in enumerate(pieces):
        loads[slot][2].wait()
        for pair in range(GQ // 2):
            piece[pair * BLOCK : (pair + 1) * BLOCK, :] = held[
                slot, 2, :, pair * PAIR : (pair + 1) * PAIR
            ]


def in_order(piece0, piece1, piece2, piece3, all_out, late_out):
    place = lax.rem(lax.axis_index("head"), ROW)
    for block in range(ROW):
        shift = lax.rem(place + ROW - block, ROW)
        value = piece0[...]
        for number, piece in enumerate((piece1, piece2, piece3)):
            value = jnp.where(shift == number + 1, piece[...], value)
        all_out[block] = value
        if block > 0:
            late_out[block - 1] = value


def stacked(piece, start):
    return jnp.concatenate(
        [
            piece[
                start + head // 2 * BLOCK : start + (head // 2 + 1) * BLOCK,
                head % 2 * DH : (head % 2 + 1) * DH,
            ]
            for head in range(GQ)
        ],
        axis=0,
    )


def side_by_side(rows):
    return jnp.concatenate([rows[pair : pair + 1] for pair in range(GQ // 2)], axis=1)


def sweep(back, doc_start, pieces, kv, dq, dkv):
    head = lax.axis_index("head")
    place = lax.rem(head, ROW)
    own_row = head // ROW
    first_key = lax.axis_index("seq") * (ROW * ROW) + (own_row - back) * ROW
    for slot, piece in pieces.items():
        query_place = lax.rem(place + ROW - slot, ROW)
        start = doc_start[own_row * ROW + query_place]

        def turn(key_slot, carry, slot=slot, piece=piece, start=start, query_place=query_place):
            key_place = key_slot + (1 if back == 2 else 0)
            seen = first_key + key_place >= start
            if back == 0:
                seen = seen & (key_place <= query_place)

            @pl.when(seen)
            def _():
                key = kv[key_slot, :, :DH]
                value = kv[key_slot, :, DH:]
                query = stacked(piece, 0)
                grad = stacked(piece, HALF)
                stats = piece[STAT:, :].astype(F32)
                norm = side_by_side(stats[0:4])
                dots = side_by_side(stats[4:8] + stats[8:12] + stats[12:16])
                weights = jnp.exp(nt(key, query) * SCALE - norm)
                if back == 0:
                    key_pos = lax.broadcasted_iota(jnp.int32, (BLOCK, WIDE), 0)
                    query_pos = lax.broadcasted_iota(jnp.int32, (BLOCK, WIDE), 1) % BLOCK
                    ahead = (query_place - key_place) * BLOCK
                    weights = jnp.where(key_pos <= query_pos + ahead, weights, 0.0)
                grad_scores = (weights * (nt(value, grad) - dots)).astype(BF16)
                dkv[key_slot, :, DH:] += nn(weights.astype(BF16), grad)
                dkv[key_slot, :, :DH] += nn(grad_scores, query)
                dq[slot] += nn(key.T, grad_scores)

            return carry

        lax.fori_loop(0, ROW - 1 if back == 2 else ROW, turn, 0)


def begin_own(doc_start, piece0, piece1, piece3, kv, dkv, dq):
    dkv[...] = jnp.zeros_like(dkv)
    for slot in (0, 1, 3):
        dq[slot] = jnp.zeros((DH, WIDE), F32)
    sweep(0, doc_start, {0: piece0, 1: piece1, 3: piece3}, kv, dq, dkv)


def begin_one(doc_start, piece0, piece1, piece3, kv, dq_in, dkv, dq):
    dkv[...] = jnp.zeros_like(dkv)
    for slot in (0, 1, 3):
        dq[slot] = dq_in[slot]
    sweep(1, doc_start, {0: piece0, 1: piece1, 3: piece3}, kv, dq, dkv)


def begin_two(doc_start, piece0, piece1, piece3, kv, dq_in, dkv, dq):
    dkv[...] = jnp.zeros_like(dkv)
    for slot in (0, 1, 3):
        dq[slot] = dq_in[slot]
    sweep(2, doc_start, {0: piece0, 1: piece1, 3: piece3}, kv, dq, dkv)


def round_kv(dkv, out):
    out[:, :, :DH] = (dkv[:, :, :DH] * SCALE).astype(BF16)
    out[:, :, DH:] = dkv[:, :, DH:].astype(BF16)


def finish_earlier(
    doc_start, piece2, kv_two, kv_one, two_in, one_in, two_out, one_out, late, two, one
):
    late[...] = jnp.zeros_like(late)
    two[...] = two_in[...]
    one[...] = one_in[...]
    sweep(2, doc_start, {2: piece2}, kv_two, Shifted(late), two)
    round_kv(two, two_out)
    sweep(1, doc_start, {2: piece2}, kv_one, Shifted(late), one)
    round_kv(one, one_out)


def finish_own(
    doc_start, piece2, kv, dkv_in, dq_in, late_in, dkv, out0, out1, out2, out3, late
):
    dkv[...] = dkv_in[...]
    late[...] = late_in[...]
    sweep(0, doc_start, {2: piece2}, kv, Shifted(late), dkv)
    dkv[:, :, :DH] = dkv[:, :, :DH] * SCALE
    for slot, out in enumerate((out0, out1, out2, out3)):
        for head in range(GQ):
            cut = slice(head * DH, (head + 1) * DH)
            total = late[0, :, cut] if slot == 2 else dq_in[slot, :, cut]
            out[:, cut] = (total.T * SCALE).astype(BF16)


class Shifted:
    def __init__(self, ref):
        self.ref = ref

    def __getitem__(self, slot):
        return self.ref[slot - 2]

    def __setitem__(self, slot, value):
        self.ref[slot - 2] = value


def add_up(own, one, two, *pieces):
    place = lax.rem(lax.axis_index("head"), ROW)
    for slot in range(ROW):
        block = lax.rem(place + ROW - slot, ROW)
        earlier = jnp.where(block > 0, two[jnp.maximum(block - 1, 0)].astype(F32), 0.0)
        pieces[slot][...] = (own[block] + one[block].astype(F32) + earlier).astype(BF16)


def join_queries(piece0, piece1, piece2, piece3, out, sems):
    place = lax.rem(lax.axis_index("head"), ROW)
    copies = []
    for shift, piece in enumerate((piece0, piece1, piece2, piece3)):
        span = pl.ds(pl.multiple_of(lax.rem(place + shift, ROW) * WIDE, WIDE), WIDE)
        copies.append(pltpu.make_async_copy(piece, out.at[:, span], sems.at[shift]))
    for copy in copies:
        copy.start()
    for copy in copies:
        copy.wait()


def join_kv(piece0, piece1, piece2, piece3, key_out, value_out, sems):
    place = lax.rem(lax.axis_index("head"), ROW)
    copies = []
    for shift, piece in enumerate((piece0, piece1, piece2, piece3)):
        columns = pl.ds(pl.multiple_of(lax.rem(place + shift, ROW) * DH, DH), DH)
        for part, out in enumerate((key_out, value_out)):
            copies.append(
                pltpu.make_async_copy(
                    piece.at[:, pl.ds(part * DH, DH)], out.at[:, columns], sems.at[shift, part]
                )
            )
    for copy in copies:
        copy.start()
    for copy in copies:
        copy.wait()


def kernel(body, name, in_specs, shapes, scratch=(), out_spec=VMEM, grant=24, cost=0):
    return pl.pallas_call(
        body,
        in_specs=in_specs,
        out_specs=[out_spec] * len(shapes),
        out_shape=[jax.ShapeDtypeStruct(*shape) for shape in shapes],
        scratch_shapes=scratch,
        compiler_params=pltpu.CompilerParams(vmem_limit_bytes=grant << 20),
        cost_estimate=pl.CostEstimate(flops=cost, bytes_accessed=cost, transcendentals=0),
        name=name,
    )


def per_device(queries, outputs, out_grads, log_norms, keys, values, doc_start):
    seqs = lax.axis_size("seq")
    heads = lax.axis_size("head")
    total = seqs * heads
    sems = pltpu.SemaphoreType.DMA

    def along_row(value, shift):
        if shift % ROW == 0:
            return value
        pairs = [(b, b - b % ROW + (b + shift) % ROW) for b in range(total)]
        return lax.ppermute(value, AXES, pairs)

    def along_rows(value, rows):
        by = rows * ROW
        return lax.ppermute(value, AXES, [(b, (b + by) % total) for b in range(total)])

    kv_shape = (ROW, BLOCK, 2 * DH)
    late_shape = (ROW - 1, BLOCK, 2 * DH)
    dq_shape = ((ROW, DH, WIDE), F32)
    piece_shape = ((PIECE, PAIR), BF16)
    turned = log_norms.T

    def pack_scratch(count):
        return [
            pltpu.VMEM((count, 3, BLOCK, WIDE), BF16),
            pltpu.VMEM((H, BLOCK), BF16),
            sems((count, 4)),
        ]

    kv_piece = ((BLOCK, 2 * DH), BF16)
    kv_sent = kernel(
        pack_kv, "pack_kv", [HBM] * 2, [kv_piece] * ROW, [sems((ROW, 2))], grant=56
    )(keys, values)
    kv_pieces = [along_row(kv_sent[shift], shift) for shift in range(ROW)]
    kv_sent, grads = lax.optimization_barrier((kv_sent, out_grads))
    near = kernel(
        functools.partial(pack, (1, 3)),
        "pack_near",
        [HBM] * 4,
        [piece_shape] * 2,
        pack_scratch(2),
        grant=52,
    )(queries, outputs, grads, turned)
    kv_pieces, near = lax.optimization_barrier((kv_pieces, near))
    piece1 = along_row(near[0], 1)
    piece3 = along_row(near[1], 3)
    kv_own, kv_late = kernel(
        in_order, "in_order", [VMEM] * ROW, [(kv_shape, BF16), (late_shape, BF16)]
    )(*kv_pieces)
    kv_one = along_rows(kv_own, 1)
    kv_two = along_rows(kv_late, 2)
    kv_own, grads_later = lax.optimization_barrier((kv_own, out_grads))
    piece0, far = kernel(
        functools.partial(pack, (0, 2)),
        "pack_rest",
        [HBM] * 4,
        [piece_shape] * 2,
        pack_scratch(2),
        grant=52,
    )(queries, outputs, grads_later, turned)
    piece1, piece3, far = lax.optimization_barrier((piece1, piece3, far))
    piece2 = along_row(far, 2)

    dkv_own, dq = kernel(
        begin_own, "begin_own", [SMEM] + [VMEM] * 4, [(kv_shape, F32), dq_shape], cost=HEAVY
    )(doc_start, piece0, piece1, piece3, kv_own)
    dkv_one, dq = kernel(
        begin_one, "begin_one", [SMEM] + [VMEM] * 5, [(kv_shape, F32), dq_shape], cost=HEAVY
    )(doc_start, piece0, piece1, piece3, kv_one, dq)
    dkv_two, dq = kernel(
        begin_two,
        "begin_two",
        [SMEM] + [VMEM] * 5,
        [(late_shape, F32), dq_shape],
        cost=HEAVY,
    )(doc_start, piece0, piece1, piece3, kv_two, dq)
    far_shape = ((1, DH, WIDE), F32)
    dkv_two, dkv_one, dq_far = kernel(
        finish_earlier,
        "finish_earlier",
        [SMEM] + [VMEM] * 5,
        [(late_shape, BF16), (kv_shape, BF16), far_shape],
        [pltpu.VMEM(late_shape, F32), pltpu.VMEM(kv_shape, F32)],
        cost=HEAVY,
    )(doc_start, piece2, kv_two, kv_one, dkv_two, dkv_one)
    back_two = along_rows(dkv_two, -2)
    back_one = along_rows(dkv_one, -1)
    dkv_own, *dq_sent = kernel(
        finish_own,
        "finish_own",
        [SMEM] + [VMEM] * 5,
        [(kv_shape, F32)] + [((BLOCK, WIDE), BF16)] * ROW,
        [pltpu.VMEM(*far_shape)],
        cost=HEAVY,
    )(doc_start, piece2, kv_own, dkv_own, dq, dq_far)
    dq_pieces = [along_row(dq_sent[slot], -slot) for slot in range(ROW)]
    (query_out,) = kernel(
        join_queries,
        "join_queries",
        [VMEM] * ROW,
        [((BLOCK, H * DH), BF16)],
        [sems((ROW,))],
        HBM,
    )(*dq_pieces)
    dkv_sent = kernel(
        add_up, "add_up", [VMEM] * 3, [((BLOCK, 2 * DH), BF16)] * ROW, cost=HEAVY
    )(
        dkv_own, back_one, back_two
    )
    dkv_pieces = [along_row(dkv_sent[slot], -slot) for slot in range(ROW)]
    key_out, value_out = kernel(
        join_kv,
        "join_kv",
        [VMEM] * ROW,
        [((BLOCK, KVH * DH), BF16)] * 2,
        [sems((ROW, 2))],
        HBM,
    )(*dkv_pieces)
    return (query_out, key_out, value_out)


def solution(mesh):
    placed = P(("seq", "head"), None)
    return jax.shard_map(
        per_device,
        mesh=mesh,
        in_specs=(placed,) * 6 + (P("seq"),),
        out_specs=(placed,) * 3,
        check_vma=False,
    )
```

profile of v0, /device:TPU:6, one launch (start us, length us, event | category | flops | bytes accessed | tf_op | source)
XLA Modules:
  0.0 76.9 jit_solution(16949347950327164044)
XLA Ops:
  0.6 1.6 %pack_kv.1 = (bf16[128,256]{1,0:T(8,128)(2,1)}, bf16[128,256]{1,0:T(8,128)(2,1)}, bf16[128,256]{1,0:T(8,128)(2,1)}, bf16[128,256]{1,0:T(8,128)(2,1)}) custom-call(bf16[128,512]{1,0:T(8,128)(2,1)} %keys.1, bf16[128,512]{1,0:T(8,128)(2,1)} %values.1), custom_call_target="tpu_custom_call" | custom-call | tf_op jit(solution)/shard_map/pack_kv/pallas_call | solution.py:335
  2.3 0.0 copy-start
  2.3 1.7 %collective-permute-start = (bf16[128,256]{1,0:T(8,128)(2,1)}, bf16[128,256]{1,0:T(8,128)(2,1)S(1)}, u32[]{:S(2)}, u32[]{:S(2)}) collective-permute-start(bf16[128,256]{1,0:T(8,128)(2,1)} %get-tuple-element.46), channel_id=1, source_target_pairs={{0,1},{1,2},{2,3},{3,0},{4,5},{5,6},{6,7},{7,4},{8,9},{9,10},{10,1... | collective-permute-start | bytes 196616 | tf_op jit(solution)/shard_map/ppermute | solution.py:315
  3.9 2.9 %collective-permute-start.1 = (bf16[128,256]{1,0:T(8,128)(2,1)}, bf16[128,256]{1,0:T(8,128)(2,1)S(1)}, u32[]{:S(2)}, u32[]{:S(2)}) collective-permute-start(bf16[128,256]{1,0:T(8,128)(2,1)} %get-tuple-element.47), channel_id=1, source_target_pairs={{0,2},{1,3},{2,0},{3,1},{4,6},{5,7},{6,4},{7,5},{8,10},{9,11},{10,... | collective-permute-start | bytes 196616 | tf_op jit(solution)/shard_map/ppermute | solution.py:315
  6.8 1.3 %collective-permute-start.2 = (bf16[128,256]{1,0:T(8,128)(2,1)}, bf16[128,256]{1,0:T(8,128)(2,1)S(1)}, u32[]{:S(2)}, u32[]{:S(2)}) collective-permute-start(bf16[128,256]{1,0:T(8,128)(2,1)} %get-tuple-element.48), channel_id=1, source_target_pairs={{0,3},{1,0},{2,1},{3,2},{4,7},{5,4},{6,5},{7,6},{8,11},{9,8},{10,9... | collective-permute-start | bytes 196616 | tf_op jit(solution)/shard_map/ppermute | solution.py:315
  8.2 0.7 copy-done.1
  8.9 2.0 %pack_near.1 = (bf16[1040,256]{1,0:T(8,128)(2,1)S(1)}, bf16[1040,256]{1,0:T(8,128)(2,1)S(1)}) custom-call(bf16[128,4096]{1,0:T(8,128)(2,1)} %queries.3, bf16[128,4096]{1,0:T(8,128)(2,1)} %outputs.3, bf16[128,4096]{1,0:T(8,128)(2,1)} %grads.1, bf16[32,128]{1,0:T(8,128)(2,1)S(1)} %bitcast.1), custom_call_target="tpu_custom_call" | custom-call | tf_op jit(solution)/shard_map/pack_near/pallas_call | solution.py:340
  10.9 0.0 copy-start.2
  10.9 0.0 collective-permute-done.piece1
  10.9 0.0 collective-permute-done.1.piece2
  10.9 0.4 collective-permute-done.2.piece3
  11.3 0.3 collective-permute-start.3
  11.7 2.9 %collective-permute-start.4 = (bf16[1040,256]{1,0:T(8,128)(2,1)S(1)}, bf16[1040,256]{1,0:T(8,128)(2,1)S(1)}, u32[]{:S(2)}, u32[]{:S(2)}) collective-permute-start(bf16[1040,256]{1,0:T(8,128)(2,1)S(1)} %get-tuple-element.53), channel_id=1, source_target_pairs={{0,3},{1,0},{2,1},{3,2},{4,7},{5,4},{6,5},{7,6},{8,11},{9,8},{10,9... | collective-permute-start | bytes 1597448 | tf_op jit(solution)/shard_map/ppermute | solution.py:315
  14.6 0.0 copy-done
  14.6 3.3 %collective-permute-start.7 = (bf16[4,128,256]{2,1,0:T(8,128)(2,1)S(1)}, bf16[4,128,256]{2,1,0:T(8,128)(2,1)S(1)}, u32[]{:S(2)}, u32[]{:S(2)}) collective-permute-start(bf16[4,128,256]{2,1,0:T(8,128)(2,1)S(1)} %get-tuple-element.62.kv), channel_id=1, source_target_pairs={{0,4},{1,5},{2,6},{3,7},{4,8},{5,9},{6,10},{7,11},{8,12},{9,13},{1... | collective-permute-start | bytes 786440 | tf_op jit(solution)/shard_map/ppermute | solution.py:319
  18.0 5.4 %collective-permute-start.6 = (bf16[3,128,256]{2,1,0:T(8,128)(2,1)S(1)}, bf16[3,128,256]{2,1,0:T(8,128)(2,1)S(1)}, u32[]{:S(2)}, u32[]{:S(2)}) collective-permute-start(bf16[3,128,256]{2,1,0:T(8,128)(2,1)S(1)} %get-tuple-element.67), channel_id=1, source_target_pairs={{0,8},{1,9},{2,10},{3,11},{4,12},{5,13},{6,14},{7,15},{8,16},{9,17... | collective-permute-start | bytes 589832 | tf_op jit(solution)/shard_map/ppermute | solution.py:319
  23.4 2.0 %pack_rest.1 = (bf16[1040,256]{1,0:T(8,128)(2,1)S(1)}, bf16[1040,256]{1,0:T(8,128)(2,1)S(1)}) custom-call(bf16[128,4096]{1,0:T(8,128)(2,1)} %queries.3, bf16[128,4096]{1,0:T(8,128)(2,1)} %outputs.3, bf16[128,4096]{1,0:T(8,128)(2,1)} %grads.1, bf16[32,128]{1,0:T(8,128)(2,1)S(1)} %bitcast.2), custom_call_target="tpu_custom_call" | custom-call | tf_op jit(solution)/shard_map/pack_rest/pallas_call | solution.py:357
  25.3 0.0 collective-permute-done.3.piece1
  25.3 0.0 collective-permute-done.4.piece3
  25.3 1.9 %collective-permute-start.5 = (bf16[1040,256]{1,0:T(8,128)(2,1)S(1)}, bf16[1040,256]{1,0:T(8,128)(2,1)S(1)}, u32[]{:S(2)}, u32[]{:S(2)}) collective-permute-start(bf16[1040,256]{1,0:T(8,128)(2,1)S(1)} %get-tuple-element.61), channel_id=1, source_target_pairs={{0,2},{1,3},{2,0},{3,1},{4,6},{5,7},{6,4},{7,5},{8,10},{9,11},{10,... | collective-permute-start | bytes 1597448 | tf_op jit(solution)/shard_map/ppermute | solution.py:315
  27.3 0.0 copy-done.2
  27.3 3.8 %begin_own.1 = (f32[4,128,256]{2,1,0:T(8,128)S(1)}, f32[4,128,1024]{2,1,0:T(8,128)S(1)}) custom-call(s32[16]{0:T(128)S(1)} %copy-done.2, bf16[1040,256]{1,0:T(8,128)(2,1)S(1)} %get-tuple-element.63.piece0, bf16[1040,256]{1,0:T(8,128)(2,1)S(1)} %collective-permute-done.3.piece1, bf16[1040,256]{1,0:T(8,128)(2,1)S(1)} %collective-permute-done.4.piece3, ...), custom_call_target="tpu_custom_call" | custom-call | flops 20000000000 | bytes 20000000000 | tf_op jit(solution)/shard_map/begin_own/pallas_call | solution.py:368
  31.1 0.0 collective-permute-done.7.kv.kv_one
  31.1 1.9 %begin_one.1 = (f32[4,128,256]{2,1,0:T(8,128)S(1)}, f32[4,128,1024]{2,1,0:T(8,128)S(1)}) custom-call(s32[16]{0:T(128)S(1)} %copy-done.2, bf16[1040,256]{1,0:T(8,128)(2,1)S(1)} %get-tuple-element.63.piece0, bf16[1040,256]{1,0:T(8,128)(2,1)S(1)} %collective-permute-done.3.piece1, bf16[1040,256]{1,0:T(8,128)(2,1)S(1)} %collective-permute-done.4.piece3, ...), custom_call_target="tpu_custom_call" | custom-call | flops 20000000000 | bytes 20000000000 | tf_op jit(solution)/shard_map/begin_one/pallas_call | solution.py:371
  33.0 0.2 collective-permute-done.6.kv.kv_two
  33.2 0.8 begin_two.1
  34.0 4.7 %collective-permute-done.5.piece2 = bf16[1040,256]{1,0:T(8,128)(2,1)S(1)} collective-permute-done((bf16[1040,256]{1,0:T(8,128)(2,1)S(1)}, bf16[1040,256]{1,0:T(8,128)(2,1)S(1)}, u32[]{:S(2)}, u32[]{:S(2)}) %collective-permute-start.5) | collective-permute-done | bytes 532512 | tf_op jit(solution)/shard_map/ppermute | solution.py:315
  38.7 0.8 %finish_earlier.1 = (bf16[3,128,256]{2,1,0:T(8,128)(2,1)S(1)}, bf16[4,128,256]{2,1,0:T(8,128)(2,1)S(1)}, f32[1,128,1024]{2,1,0:T(8,128)S(1)}) custom-call(s32[16]{0:T(128)S(1)} %copy-done.2, bf16[1040,256]{1,0:T(8,128)(2,1)S(1)} %collective-permute-done.5.piece2, bf16[3,128,256]{2,1,0:T(8,128)(2,1)S(1)} %collective-permute-done.6.kv.kv_two, ...), custom_call_target="tpu_custom_call" | custom-call | flops 20000000000 | bytes 20000000000 | tf_op jit(solution)/shard_map/finish_earlier/pallas_call | solution.py:382
  39.4 3.7 %collective-permute-start.12 = (bf16[3,128,256]{2,1,0:T(8,128)(2,1)S(1)}, bf16[3,128,256]{2,1,0:T(8,128)(2,1)S(1)}, u32[]{:S(2)}, u32[]{:S(2)}) collective-permute-start(bf16[3,128,256]{2,1,0:T(8,128)(2,1)S(1)} %get-tuple-element.80), channel_id=1, source_target_pairs={{0,248},{1,249},{2,250},{3,251},{4,252},{5,253},{6,254},{7,255},{8... | collective-permute-start | bytes 589832 | tf_op jit(solution)/shard_map/ppermute | solution.py:319
  43.2 5.0 %collective-permute-start.11 = (bf16[4,128,256]{2,1,0:T(8,128)(2,1)S(1)}, bf16[4,128,256]{2,1,0:T(8,128)(2,1)S(1)}, u32[]{:S(2)}, u32[]{:S(2)}) collective-permute-start(bf16[4,128,256]{2,1,0:T(8,128)(2,1)S(1)} %get-tuple-element.79), channel_id=1, source_target_pairs={{0,252},{1,253},{2,254},{3,255},{4,0},{5,1},{6,2},{7,3},{8,4},{9,5... | collective-permute-start | bytes 786440 | tf_op jit(solution)/shard_map/ppermute | solution.py:319
  48.1 1.9 %finish_own.1 = (f32[4,128,256]{2,1,0:T(8,128)S(1)}, bf16[128,1024]{1,0:T(8,128)(2,1)S(1)}, bf16[128,1024]{1,0:T(8,128)(2,1)S(1)}, bf16[128,1024]{1,0:T(8,128)(2,1)S(1)}, bf16[128,1024]{1,0:T(8,128)(2,1)S(1)}) custom-call(s32[16]{0:T(128)S(1)} %copy-done.2, bf16[1040,256]{1,0:T(8,128)(2,1)S(1)} %collective-permute-done.5.piece2, ...), custom_call_target="tpu_custom_call" | custom-call | flops 20000000000 | bytes 20000000000 | tf_op jit(solution)/shard_map/finish_own/pallas_call | solution.py:392
  50.0 4.1 %collective-permute-start.8 = (bf16[128,1024]{1,0:T(8,128)(2,1)S(1)}, bf16[128,1024]{1,0:T(8,128)(2,1)S(1)}, u32[]{:S(2)}, u32[]{:S(2)}) collective-permute-start(bf16[128,1024]{1,0:T(8,128)(2,1)S(1)} %get-tuple-element.75), channel_id=1, source_target_pairs={{0,3},{1,0},{2,1},{3,2},{4,7},{5,4},{6,5},{7,6},{8,11},{9,8},{10,9... | collective-permute-start | bytes 786440 | tf_op jit(solution)/shard_map/ppermute | solution.py:315
  54.1 0.0 collective-permute-start.9
  54.1 1.0 %collective-permute-start.10 = (bf16[128,1024]{1,0:T(8,128)(2,1)S(1)}, bf16[128,1024]{1,0:T(8,128)(2,1)S(1)}, u32[]{:S(2)}, u32[]{:S(2)}) collective-permute-start(bf16[128,1024]{1,0:T(8,128)(2,1)S(1)} %get-tuple-element.77), channel_id=1, source_target_pairs={{0,1},{1,2},{2,3},{3,0},{4,5},{5,6},{6,7},{7,4},{8,9},{9,10},{10,1... | collective-permute-start | bytes 786440 | tf_op jit(solution)/shard_map/ppermute | solution.py:315
  55.1 0.0 collective-permute-done.12.two
  55.1 12.0 %collective-permute-done.11.one = bf16[4,128,256]{2,1,0:T(8,128)(2,1)S(1)} collective-permute-done((bf16[4,128,256]{2,1,0:T(8,128)(2,1)S(1)}, bf16[4,128,256]{2,1,0:T(8,128)(2,1)S(1)}, u32[]{:S(2)}, u32[]{:S(2)}) %collective-permute-start.11) | collective-permute-done | bytes 262176 | tf_op jit(solution)/shard_map/ppermute | solution.py:319
  67.1 0.1 add_up.1
  67.2 2.3 %collective-permute-start.13 = (bf16[128,256]{1,0:T(8,128)(2,1)S(1)}, bf16[128,256]{1,0:T(8,128)(2,1)S(1)}, u32[]{:S(2)}, u32[]{:S(2)}) collective-permute-start(bf16[128,256]{1,0:T(8,128)(2,1)S(1)} %get-tuple-element.82), channel_id=1, source_target_pairs={{0,3},{1,0},{2,1},{3,2},{4,7},{5,4},{6,5},{7,6},{8,11},{9,8},{10,9... | collective-permute-start | bytes 196616 | tf_op jit(solution)/shard_map/ppermute | solution.py:315
  69.5 0.0 collective-permute-start.14
  69.5 0.0 collective-permute-done.8.piece1
  69.5 1.0 %collective-permute-start.15 = (bf16[128,256]{1,0:T(8,128)(2,1)S(1)}, bf16[128,256]{1,0:T(8,128)(2,1)S(1)}, u32[]{:S(2)}, u32[]{:S(2)}) collective-permute-start(bf16[128,256]{1,0:T(8,128)(2,1)S(1)} %get-tuple-element.84), channel_id=1, source_target_pairs={{0,1},{1,2},{2,3},{3,0},{4,5},{5,6},{6,7},{7,4},{8,9},{9,10},{10,1... | collective-permute-start | bytes 196616 | tf_op jit(solution)/shard_map/ppermute | solution.py:315
  70.4 0.0 collective-permute-done.9.piece2
  70.4 0.0 collective-permute-done.10.piece3
  70.4 1.0 %join_queries.1 = bf16[128,4096]{1,0:T(8,128)(2,1)} custom-call(bf16[128,1024]{1,0:T(8,128)(2,1)S(1)} %get-tuple-element.74.piece0, bf16[128,1024]{1,0:T(8,128)(2,1)S(1)} %collective-permute-done.8.piece1, bf16[128,1024]{1,0:T(8,128)(2,1)S(1)} %collective-permute-done.9.piece2, bf16[128,1024]{1,0:T(8,128)(2,1)S(1)} %collective-permute-done.10.piece3), custom_call_target="tpu_custom_call" | custom-call | tf_op jit(solution)/shard_map/join_queries/pallas_call | solution.py:401
  71.5 1.2 %collective-permute-done.13.piece1 = bf16[128,256]{1,0:T(8,128)(2,1)S(1)} collective-permute-done((bf16[128,256]{1,0:T(8,128)(2,1)S(1)}, bf16[128,256]{1,0:T(8,128)(2,1)S(1)}, u32[]{:S(2)}, u32[]{:S(2)}) %collective-permute-start.13) | collective-permute-done | bytes 65568 | tf_op jit(solution)/shard_map/ppermute | solution.py:315
  72.6 3.0 %collective-permute-done.14.piece2 = bf16[128,256]{1,0:T(8,128)(2,1)S(1)} collective-permute-done((bf16[128,256]{1,0:T(8,128)(2,1)S(1)}, bf16[128,256]{1,0:T(8,128)(2,1)S(1)}, u32[]{:S(2)}, u32[]{:S(2)}) %collective-permute-start.14) | collective-permute-done | bytes 65568 | tf_op jit(solution)/shard_map/ppermute | solution.py:315
  75.6 0.4 collective-permute-done.15.piece3
  75.9 0.8 join_kv.1
  (2 shorter events, 0.0 us)
Async XLA Ops:
  2.3 12.3 %copy-start = (bf16[128,256]{1,0:T(8,128)(2,1)S(1)}, bf16[128,256]{1,0:T(8,128)(2,1)}, u32[]{:S(2)}) copy-start(bf16[128,256]{1,0:T(8,128)(2,1)} %get-tuple-element.54.piece0) | copy-start | bytes 196612
  2.3 8.6 %collective-permute-start = (bf16[128,256]{1,0:T(8,128)(2,1)}, bf16[128,256]{1,0:T(8,128)(2,1)S(1)}, u32[]{:S(2)}, u32[]{:S(2)}) collective-permute-start(bf16[128,256]{1,0:T(8,128)(2,1)} %get-tuple-element.46), channel_id=1, source_target_pairs={{0,1},{1,2},{2,3},{3,0},{4,5},{5,6},{6,7},{7,4},{8,9},{9,10},{10,1... | collective-permute-start | bytes 196616 | tf_op jit(solution)/shard_map/ppermute | solution.py:315
  3.9 6.9 %collective-permute-start.1 = (bf16[128,256]{1,0:T(8,128)(2,1)}, bf16[128,256]{1,0:T(8,128)(2,1)S(1)}, u32[]{:S(2)}, u32[]{:S(2)}) collective-permute-start(bf16[128,256]{1,0:T(8,128)(2,1)} %get-tuple-element.47), channel_id=1, source_target_pairs={{0,2},{1,3},{2,0},{3,1},{4,6},{5,7},{6,4},{7,5},{8,10},{9,11},{10,... | collective-permute-start | bytes 196616 | tf_op jit(solution)/shard_map/ppermute | solution.py:315
  6.8 4.5 %collective-permute-start.2 = (bf16[128,256]{1,0:T(8,128)(2,1)}, bf16[128,256]{1,0:T(8,128)(2,1)S(1)}, u32[]{:S(2)}, u32[]{:S(2)}) collective-permute-start(bf16[128,256]{1,0:T(8,128)(2,1)} %get-tuple-element.48), channel_id=1, source_target_pairs={{0,3},{1,0},{2,1},{3,2},{4,7},{5,4},{6,5},{7,6},{8,11},{9,8},{10,9... | collective-permute-start | bytes 196616 | tf_op jit(solution)/shard_map/ppermute | solution.py:315
  8.2 0.7 copy-start.1
  10.9 16.4 %copy-start.2 = (s32[16]{0:T(128)S(1)}, s32[16]{0:T(128)}, u32[]{:S(2)}) copy-start(s32[16]{0:T(128)} %doc_start.9) | copy-start | bytes 196
  11.3 14.0 %collective-permute-start.3 = (bf16[1040,256]{1,0:T(8,128)(2,1)S(1)}, bf16[1040,256]{1,0:T(8,128)(2,1)S(1)}, u32[]{:S(2)}, u32[]{:S(2)}) collective-permute-start(bf16[1040,256]{1,0:T(8,128)(2,1)S(1)} %get-tuple-element.52), channel_id=1, source_target_pairs={{0,1},{1,2},{2,3},{3,0},{4,5},{5,6},{6,7},{7,4},{8,9},{9,10},{10,1... | collective-permute-start | bytes 1597448 | tf_op jit(solution)/shard_map/ppermute | solution.py:315
  11.7 13.7 %collective-permute-start.4 = (bf16[1040,256]{1,0:T(8,128)(2,1)S(1)}, bf16[1040,256]{1,0:T(8,128)(2,1)S(1)}, u32[]{:S(2)}, u32[]{:S(2)}) collective-permute-start(bf16[1040,256]{1,0:T(8,128)(2,1)S(1)} %get-tuple-element.53), channel_id=1, source_target_pairs={{0,3},{1,0},{2,1},{3,2},{4,7},{5,4},{6,5},{7,6},{8,11},{9,8},{10,9... | collective-permute-start | bytes 1597448 | tf_op jit(solution)/shard_map/ppermute | solution.py:315
  14.6 16.5 %collective-permute-start.7 = (bf16[4,128,256]{2,1,0:T(8,128)(2,1)S(1)}, bf16[4,128,256]{2,1,0:T(8,128)(2,1)S(1)}, u32[]{:S(2)}, u32[]{:S(2)}) collective-permute-start(bf16[4,128,256]{2,1,0:T(8,128)(2,1)S(1)} %get-tuple-element.62.kv), channel_id=1, source_target_pairs={{0,4},{1,5},{2,6},{3,7},{4,8},{5,9},{6,10},{7,11},{8,12},{9,13},{1... | collective-permute-start | bytes 786440 | tf_op jit(solution)/shard_map/ppermute | solution.py:319
  18.0 15.2 %collective-permute-start.6 = (bf16[3,128,256]{2,1,0:T(8,128)(2,1)S(1)}, bf16[3,128,256]{2,1,0:T(8,128)(2,1)S(1)}, u32[]{:S(2)}, u32[]{:S(2)}) collective-permute-start(bf16[3,128,256]{2,1,0:T(8,128)(2,1)S(1)} %get-tuple-element.67), channel_id=1, source_target_pairs={{0,8},{1,9},{2,10},{3,11},{4,12},{5,13},{6,14},{7,15},{8,16},{9,17... | collective-permute-start | bytes 589832 | tf_op jit(solution)/shard_map/ppermute | solution.py:319
  25.3 13.3 %collective-permute-start.5 = (bf16[1040,256]{1,0:T(8,128)(2,1)S(1)}, bf16[1040,256]{1,0:T(8,128)(2,1)S(1)}, u32[]{:S(2)}, u32[]{:S(2)}) collective-permute-start(bf16[1040,256]{1,0:T(8,128)(2,1)S(1)} %get-tuple-element.61), channel_id=1, source_target_pairs={{0,2},{1,3},{2,0},{3,1},{4,6},{5,7},{6,4},{7,5},{8,10},{9,11},{10,... | collective-permute-start | bytes 1597448 | tf_op jit(solution)/shard_map/ppermute | solution.py:315
  39.4 15.6 %collective-permute-start.12 = (bf16[3,128,256]{2,1,0:T(8,128)(2,1)S(1)}, bf16[3,128,256]{2,1,0:T(8,128)(2,1)S(1)}, u32[]{:S(2)}, u32[]{:S(2)}) collective-permute-start(bf16[3,128,256]{2,1,0:T(8,128)(2,1)S(1)} %get-tuple-element.80), channel_id=1, source_target_pairs={{0,248},{1,249},{2,250},{3,251},{4,252},{5,253},{6,254},{7,255},{8... | collective-permute-start | bytes 589832 | tf_op jit(solution)/shard_map/ppermute | solution.py:319
  43.2 23.9 %collective-permute-start.11 = (bf16[4,128,256]{2,1,0:T(8,128)(2,1)S(1)}, bf16[4,128,256]{2,1,0:T(8,128)(2,1)S(1)}, u32[]{:S(2)}, u32[]{:S(2)}) collective-permute-start(bf16[4,128,256]{2,1,0:T(8,128)(2,1)S(1)} %get-tuple-element.79), channel_id=1, source_target_pairs={{0,252},{1,253},{2,254},{3,255},{4,0},{5,1},{6,2},{7,3},{8,4},{9,5... | collective-permute-start | bytes 786440 | tf_op jit(solution)/shard_map/ppermute | solution.py:319
  50.0 19.5 %collective-permute-start.8 = (bf16[128,1024]{1,0:T(8,128)(2,1)S(1)}, bf16[128,1024]{1,0:T(8,128)(2,1)S(1)}, u32[]{:S(2)}, u32[]{:S(2)}) collective-permute-start(bf16[128,1024]{1,0:T(8,128)(2,1)S(1)} %get-tuple-element.75), channel_id=1, source_target_pairs={{0,3},{1,0},{2,1},{3,2},{4,7},{5,4},{6,5},{7,6},{8,11},{9,8},{10,9... | collective-permute-start | bytes 786440 | tf_op jit(solution)/shard_map/ppermute | solution.py:315
  54.1 16.3 %collective-permute-start.9 = (bf16[128,1024]{1,0:T(8,128)(2,1)S(1)}, bf16[128,1024]{1,0:T(8,128)(2,1)S(1)}, u32[]{:S(2)}, u32[]{:S(2)}) collective-permute-start(bf16[128,1024]{1,0:T(8,128)(2,1)S(1)} %get-tuple-element.76), channel_id=1, source_target_pairs={{0,2},{1,3},{2,0},{3,1},{4,6},{5,7},{6,4},{7,5},{8,10},{9,11},{10,... | collective-permute-start | bytes 786440 | tf_op jit(solution)/shard_map/ppermute | solution.py:315
  54.1 16.3 %collective-permute-start.10 = (bf16[128,1024]{1,0:T(8,128)(2,1)S(1)}, bf16[128,1024]{1,0:T(8,128)(2,1)S(1)}, u32[]{:S(2)}, u32[]{:S(2)}) collective-permute-start(bf16[128,1024]{1,0:T(8,128)(2,1)S(1)} %get-tuple-element.77), channel_id=1, source_target_pairs={{0,1},{1,2},{2,3},{3,0},{4,5},{5,6},{6,7},{7,4},{8,9},{9,10},{10,1... | collective-permute-start | bytes 786440 | tf_op jit(solution)/shard_map/ppermute | solution.py:315
  67.2 5.5 %collective-permute-start.13 = (bf16[128,256]{1,0:T(8,128)(2,1)S(1)}, bf16[128,256]{1,0:T(8,128)(2,1)S(1)}, u32[]{:S(2)}, u32[]{:S(2)}) collective-permute-start(bf16[128,256]{1,0:T(8,128)(2,1)S(1)} %get-tuple-element.82), channel_id=1, source_target_pairs={{0,3},{1,0},{2,1},{3,2},{4,7},{5,4},{6,5},{7,6},{8,11},{9,8},{10,9... | collective-permute-start | bytes 196616 | tf_op jit(solution)/shard_map/ppermute | solution.py:315
  69.5 6.1 %collective-permute-start.14 = (bf16[128,256]{1,0:T(8,128)(2,1)S(1)}, bf16[128,256]{1,0:T(8,128)(2,1)S(1)}, u32[]{:S(2)}, u32[]{:S(2)}) collective-permute-start(bf16[128,256]{1,0:T(8,128)(2,1)S(1)} %get-tuple-element.83), channel_id=1, source_target_pairs={{0,2},{1,3},{2,0},{3,1},{4,6},{5,7},{6,4},{7,5},{8,10},{9,11},{10,... | collective-permute-start | bytes 196616 | tf_op jit(solution)/shard_map/ppermute | solution.py:315
  69.5 6.4 %collective-permute-start.15 = (bf16[128,256]{1,0:T(8,128)(2,1)S(1)}, bf16[128,256]{1,0:T(8,128)(2,1)S(1)}, u32[]{:S(2)}, u32[]{:S(2)}) collective-permute-start(bf16[128,256]{1,0:T(8,128)(2,1)S(1)} %get-tuple-element.84), channel_id=1, source_target_pairs={{0,1},{1,2},{2,3},{3,0},{4,5},{5,6},{6,7},{7,4},{8,9},{9,10},{10,1... | collective-permute-start | bytes 196616 | tf_op jit(solution)/shard_map/ppermute | solution.py:315
where the time goes:
time: 77.7 us; the launch traced here: 76.9 us
  starting transfers between devices  36.9 us (47%)
  waiting for transfers between devices  21.8 us (28%)
  Pallas kernels  16.5 us (21%)
  between operations  0.94 us (1%)
    ppermute x12, starting transfers between devices, along_row(): return lax.ppermute(value, AXES, pairs)  19.4 us
    ppermute x4, starting transfers between devices, along_rows(): lax.ppermute(value, AXES, [(b, (b + by) % total) for b in range(total)])  17.5 us
    ppermute x4, waiting for transfers between devices, along_rows(): lax.ppermute(value, AXES, [(b, (b + by) % total) for b in range(total)])  12.2 us
    ppermute x12, waiting for transfers between devices, along_row(): return lax.ppermute(value, AXES, pairs)  9.6 us
    pallas_call x1, Pallas kernels, per_device(): kernel(begin_own, 'begin_own', [SMEM] + [VMEM] * 4, [(kv_shape, F32), dq_...  3.83 us
    pallas_call x1, Pallas kernels, per_device(): kernel(functools.partial(pack, (0, 2)), 'pack_rest', [HBM] * 4, [piece_sh...  1.95 us
    pallas_call x1, Pallas kernels, per_device(): kernel(functools.partial(pack, (1, 3)), 'pack_near', [HBM] * 4, [piece_sh...  1.95 us
    pallas_call x1, Pallas kernels, per_device(): kernel(finish_own, 'finish_own', [SMEM] + [VMEM] * 5, [(kv_shape, F32)] +...  1.86 us
  transfers between devices with their start and end apart: 16, of which 7 were waited for; matrix products, arithmetic and copies ran while one was open for 0% of the time, Pallas kernels for 17%

commit v1 on v0

--- a/solution.py
+++ b/solution.py
@@ -203,28 +203,28 @@
     sweep(1, doc_start, {0: piece0, 1: piece1, 3: piece3}, kv, dq, dkv)
 
 
-def begin_two(doc_start, piece0, piece1, piece3, kv, dq_in, dkv, dq):
-    dkv[...] = jnp.zeros_like(dkv)
-    for slot in (0, 1, 3):
-        dq[slot] = dq_in[slot]
-    sweep(2, doc_start, {0: piece0, 1: piece1, 3: piece3}, kv, dq, dkv)
-
-
 def round_kv(dkv, out):
     out[:, :, :DH] = (dkv[:, :, :DH] * SCALE).astype(BF16)
     out[:, :, DH:] = dkv[:, :, DH:].astype(BF16)
 
 
-def finish_earlier(
-    doc_start, piece2, kv_two, kv_one, two_in, one_in, two_out, one_out, late, two, one
+def finish_one(doc_start, piece2, kv, one_in, out, late, one):
+    late[...] = jnp.zeros_like(late)
+    one[...] = one_in[...]
+    sweep(1, doc_start, {2: piece2}, kv, Shifted(late), one)
+    round_kv(one, out)
+
+
+def all_two(
+    doc_start, piece0, piece1, piece2, piece3, kv, dq_in, late_in, out, dq, late, two
 ):
-    late[...] = jnp.zeros_like(late)
-    two[...] = two_in[...]
-    one[...] = one_in[...]
-    sweep(2, doc_start, {2: piece2}, kv_two, Shifted(late), two)
-    round_kv(two, two_out)
-    sweep(1, doc_start, {2: piece2}, kv_one, Shifted(late), one)
-    round_kv(one, one_out)
+    two[...] = jnp.zeros_like(two)
+    late[...] = late_in[...]
+    for slot in (0, 1, 3):
+        dq[slot] = dq_in[slot]
+    sweep(2, doc_start, {0: piece0, 1: piece1, 3: piece3}, kv, dq, two)
+    sweep(2, doc_start, {2: piece2}, kv, Shifted(late), two)
+    round_kv(two, out)
 
 
 def finish_own(
@@ -371,22 +371,23 @@
     dkv_one, dq = kernel(
         begin_one, "begin_one", [SMEM] + [VMEM] * 5, [(kv_shape, F32), dq_shape], cost=HEAVY
     )(doc_start, piece0, piece1, piece3, kv_one, dq)
-    dkv_two, dq = kernel(
-        begin_two,
-        "begin_two",
-        [SMEM] + [VMEM] * 5,
-        [(late_shape, F32), dq_shape],
+    far_shape = ((1, DH, WIDE), F32)
+    dkv_one, dq_far = kernel(
+        finish_one,
+        "finish_one",
+        [SMEM] + [VMEM] * 3,
+        [(kv_shape, BF16), far_shape],
+        [pltpu.VMEM(kv_shape, F32)],
         cost=HEAVY,
-    )(doc_start, piece0, piece1, piece3, kv_two, dq)
-    far_shape = ((1, DH, WIDE), F32)
-    dkv_two, dkv_one, dq_far = kernel(
-        finish_earlier,
-        "finish_earlier",
-        [SMEM] + [VMEM] * 5,
-        [(late_shape, BF16), (kv_shape, BF16), far_shape],
-        [pltpu.VMEM(late_shape, F32), pltpu.VMEM(kv_shape, F32)],
+    )(doc_start, piece2, kv_one, dkv_one)
+    dkv_two, dq, dq_far = kernel(
+        all_two,
+        "all_two",
+        [SMEM] + [VMEM] * 7,
+        [(late_shape, BF16), dq_shape, far_shape],
+        [pltpu.VMEM(late_shape, F32)],
         cost=HEAVY,
-    )(doc_start, piece2, kv_two, kv_one, dkv_two, dkv_one)
+    )(doc_start, piece0, piece1, piece2, piece3, kv_two, dq, dq_far)
     back_two = along_rows(dkv_two, -2)
     back_one = along_rows(dkv_one, -1)
     dkv_own, *dq_sent = kernel(
@@ -395,7 +396,7 @@
         [SMEM] + [VMEM] * 5,
         [(kv_shape, F32)] + [((BLOCK, WIDE), BF16)] * ROW,
         [pltpu.VMEM(*far_shape)],
-        cost=HEAVY,
+        cost=0,
     )(doc_start, piece2, kv_own, dkv_own, dq, dq_far)
     dq_pieces = [along_row(dq_sent[slot], -slot) for slot in range(ROW)]
     (query_out,) = kernel(

time: 77.7 us -> 75.6 us (0.973)
  the two profiles are of different devices: /device:TPU:6 before, /device:TPU:32 now
where the time goes in v1:
time: 75.6 us; the launch traced here: 74.8 us
  starting transfers between devices  30.2 us (40%)
  waiting for transfers between devices  22 us (29%)
  Pallas kernels  20.9 us (28%)
  between operations  0.93 us (1%)
    ppermute x12, starting transfers between devices, along_row(): return lax.ppermute(value, AXES, pairs)  19.1 us
    ppermute x4, waiting for transfers between devices, along_rows(): lax.ppermute(value, AXES, [(b, (b + by) % total) for b in range(total)])  14.5 us
    ppermute x4, starting transfers between devices, along_rows(): lax.ppermute(value, AXES, [(b, (b + by) % total) for b in range(total)])  11.1 us
    ppermute x12, waiting for transfers between devices, along_row(): return lax.ppermute(value, AXES, pairs)  7.55 us
    pallas_call x1, Pallas kernels, per_device(): kernel(begin_one, 'begin_one', [SMEM] + [VMEM] * 5, [(kv_shape, F32), dq_...  3.95 us
    pallas_call x1, Pallas kernels, per_device(): kernel(begin_own, 'begin_own', [SMEM] + [VMEM] * 4, [(kv_shape, F32), dq_...  3.25 us
    pallas_call x1, Pallas kernels, per_device(): kernel(finish_own, 'finish_own', [SMEM] + [VMEM] * 5, [(kv_shape, F32)] +...  3.08 us
    pallas_call x1, Pallas kernels, per_device(): kernel(finish_one, 'finish_one', [SMEM] + [VMEM] * 3, [(kv_shape, BF16),...  2.25 us
  transfers between devices with their start and end apart: 16, of which 8 were waited for; matrix products, arithmetic and copies ran while one was open for 0% of the time, Pallas kernels for 25%

profile of v1, /device:TPU:32, one launch (start us, length us, event | category | flops | bytes accessed | tf_op | source)
XLA Modules:
  0.0 74.8 jit_solution(14107309133633636795)
XLA Ops:
  0.6 1.6 %pack_kv.1 = (bf16[128,256]{1,0:T(8,128)(2,1)}, bf16[128,256]{1,0:T(8,128)(2,1)}, bf16[128,256]{1,0:T(8,128)(2,1)}, bf16[128,256]{1,0:T(8,128)(2,1)}) custom-call(bf16[128,512]{1,0:T(8,128)(2,1)} %keys.1, bf16[128,512]{1,0:T(8,128)(2,1)} %values.1), custom_call_target="tpu_custom_call" | custom-call | tf_op jit(solution)/shard_map/pack_kv/pallas_call | solution.py:335
  2.3 0.0 copy-start
  2.3 1.7 %collective-permute-start = (bf16[128,256]{1,0:T(8,128)(2,1)}, bf16[128,256]{1,0:T(8,128)(2,1)S(1)}, u32[]{:S(2)}, u32[]{:S(2)}) collective-permute-start(bf16[128,256]{1,0:T(8,128)(2,1)} %get-tuple-element.46), channel_id=1, source_target_pairs={{0,1},{1,2},{2,3},{3,0},{4,5},{5,6},{6,7},{7,4},{8,9},{9,10},{10,1... | collective-permute-start | bytes 196616 | tf_op jit(solution)/shard_map/ppermute | solution.py:315
  3.9 2.9 %collective-permute-start.1 = (bf16[128,256]{1,0:T(8,128)(2,1)}, bf16[128,256]{1,0:T(8,128)(2,1)S(1)}, u32[]{:S(2)}, u32[]{:S(2)}) collective-permute-start(bf16[128,256]{1,0:T(8,128)(2,1)} %get-tuple-element.47), channel_id=1, source_target_pairs={{0,2},{1,3},{2,0},{3,1},{4,6},{5,7},{6,4},{7,5},{8,10},{9,11},{10,... | collective-permute-start | bytes 196616 | tf_op jit(solution)/shard_map/ppermute | solution.py:315
  6.8 1.3 %collective-permute-start.2 = (bf16[128,256]{1,0:T(8,128)(2,1)}, bf16[128,256]{1,0:T(8,128)(2,1)S(1)}, u32[]{:S(2)}, u32[]{:S(2)}) collective-permute-start(bf16[128,256]{1,0:T(8,128)(2,1)} %get-tuple-element.48), channel_id=1, source_target_pairs={{0,3},{1,0},{2,1},{3,2},{4,7},{5,4},{6,5},{7,6},{8,11},{9,8},{10,9... | collective-permute-start | bytes 196616 | tf_op jit(solution)/shard_map/ppermute | solution.py:315
  8.2 0.7 copy-done.1
  8.9 2.0 %pack_near.1 = (bf16[1040,256]{1,0:T(8,128)(2,1)S(1)}, bf16[1040,256]{1,0:T(8,128)(2,1)S(1)}) custom-call(bf16[128,4096]{1,0:T(8,128)(2,1)} %queries.3, bf16[128,4096]{1,0:T(8,128)(2,1)} %outputs.3, bf16[128,4096]{1,0:T(8,128)(2,1)} %grads.1, bf16[32,128]{1,0:T(8,128)(2,1)S(1)} %bitcast.1), custom_call_target="tpu_custom_call" | custom-call | tf_op jit(solution)/shard_map/pack_near/pallas_call | solution.py:340
  10.9 0.0 copy-start.2
  10.9 0.0 collective-permute-done.piece1
  10.9 0.0 collective-permute-done.1.piece2
  10.9 0.4 collective-permute-done.2.piece3
  11.3 0.3 collective-permute-start.3
  11.7 2.9 %collective-permute-start.4 = (bf16[1040,256]{1,0:T(8,128)(2,1)S(1)}, bf16[1040,256]{1,0:T(8,128)(2,1)S(1)}, u32[]{:S(2)}, u32[]{:S(2)}) collective-permute-start(bf16[1040,256]{1,0:T(8,128)(2,1)S(1)} %get-tuple-element.53), channel_id=1, source_target_pairs={{0,3},{1,0},{2,1},{3,2},{4,7},{5,4},{6,5},{7,6},{8,11},{9,8},{10,9... | collective-permute-start | bytes 1597448 | tf_op jit(solution)/shard_map/ppermute | solution.py:315
  14.6 0.0 copy-done
  14.6 3.3 %collective-permute-start.7 = (bf16[4,128,256]{2,1,0:T(8,128)(2,1)S(1)}, bf16[4,128,256]{2,1,0:T(8,128)(2,1)S(1)}, u32[]{:S(2)}, u32[]{:S(2)}) collective-permute-start(bf16[4,128,256]{2,1,0:T(8,128)(2,1)S(1)} %get-tuple-element.62.kv), channel_id=1, source_target_pairs={{0,4},{1,5},{2,6},{3,7},{4,8},{5,9},{6,10},{7,11},{8,12},{9,13},{1... | collective-permute-start | bytes 786440 | tf_op jit(solution)/shard_map/ppermute | solution.py:319
  18.0 4.5 %collective-permute-start.6 = (bf16[3,128,256]{2,1,0:T(8,128)(2,1)S(1)}, bf16[3,128,256]{2,1,0:T(8,128)(2,1)S(1)}, u32[]{:S(2)}, u32[]{:S(2)}) collective-permute-start(bf16[3,128,256]{2,1,0:T(8,128)(2,1)S(1)} %get-tuple-element.67), channel_id=1, source_target_pairs={{0,8},{1,9},{2,10},{3,11},{4,12},{5,13},{6,14},{7,15},{8,16},{9,17... | collective-permute-start | bytes 589832 | tf_op jit(solution)/shard_map/ppermute | solution.py:319
  22.5 2.0 %pack_rest.1 = (bf16[1040,256]{1,0:T(8,128)(2,1)S(1)}, bf16[1040,256]{1,0:T(8,128)(2,1)S(1)}) custom-call(bf16[128,4096]{1,0:T(8,128)(2,1)} %queries.3, bf16[128,4096]{1,0:T(8,128)(2,1)} %outputs.3, bf16[128,4096]{1,0:T(8,128)(2,1)} %grads.1, bf16[32,128]{1,0:T(8,128)(2,1)S(1)} %bitcast.2), custom_call_target="tpu_custom_call" | custom-call | tf_op jit(solution)/shard_map/pack_rest/pallas_call | solution.py:357
  24.4 0.8 %collective-permute-done.3.piece1 = bf16[1040,256]{1,0:T(8,128)(2,1)S(1)} collective-permute-done((bf16[1040,256]{1,0:T(8,128)(2,1)S(1)}, bf16[1040,256]{1,0:T(8,128)(2,1)S(1)}, u32[]{:S(2)}, u32[]{:S(2)}) %collective-permute-start.3) | collective-permute-done | bytes 532512 | tf_op jit(solution)/shard_map/ppermute | solution.py:315
  25.2 0.0 collective-permute-done.4.piece3
  25.2 2.1 %collective-permute-start.5 = (bf16[1040,256]{1,0:T(8,128)(2,1)S(1)}, bf16[1040,256]{1,0:T(8,128)(2,1)S(1)}, u32[]{:S(2)}, u32[]{:S(2)}) collective-permute-start(bf16[1040,256]{1,0:T(8,128)(2,1)S(1)} %get-tuple-element.61), channel_id=1, source_target_pairs={{0,2},{1,3},{2,0},{3,1},{4,6},{5,7},{6,4},{7,5},{8,10},{9,11},{10,... | collective-permute-start | bytes 1597448 | tf_op jit(solution)/shard_map/ppermute | solution.py:315
  27.3 0.0 copy-done.2
  27.3 3.2 %begin_own.1 = (f32[4,128,256]{2,1,0:T(8,128)S(1)}, f32[4,128,1024]{2,1,0:T(8,128)S(1)}) custom-call(s32[16]{0:T(128)S(1)} %copy-done.2, bf16[1040,256]{1,0:T(8,128)(2,1)S(1)} %get-tuple-element.63.piece0, bf16[1040,256]{1,0:T(8,128)(2,1)S(1)} %collective-permute-done.3.piece1, bf16[1040,256]{1,0:T(8,128)(2,1)S(1)} %collective-permute-done.4.piece3, ...), custom_call_target="tpu_custom_call" | custom-call | flops 20000000000 | bytes 20000000000 | tf_op jit(solution)/shard_map/begin_own/pallas_call | solution.py:368
  30.6 1.8 %collective-permute-done.7.kv = bf16[4,128,256]{2,1,0:T(8,128)(2,1)S(1)} collective-permute-done((bf16[4,128,256]{2,1,0:T(8,128)(2,1)S(1)}, bf16[4,128,256]{2,1,0:T(8,128)(2,1)S(1)}, u32[]{:S(2)}, u32[]{:S(2)}) %collective-permute-start.7) | collective-permute-done | bytes 262176 | tf_op jit(solution)/shard_map/ppermute | solution.py:319
  32.3 4.0 %begin_one.1 = (f32[4,128,256]{2,1,0:T(8,128)S(1)}, f32[4,128,1024]{2,1,0:T(8,128)S(1)}) custom-call(s32[16]{0:T(128)S(1)} %copy-done.2, bf16[1040,256]{1,0:T(8,128)(2,1)S(1)} %get-tuple-element.63.piece0, bf16[1040,256]{1,0:T(8,128)(2,1)S(1)} %collective-permute-done.3.piece1, bf16[1040,256]{1,0:T(8,128)(2,1)S(1)} %collective-permute-done.4.piece3, ...), custom_call_target="tpu_custom_call" | custom-call | flops 20000000000 | bytes 20000000000 | tf_op jit(solution)/shard_map/begin_one/pallas_call | solution.py:371
  36.3 2.1 %collective-permute-done.5.piece2 = bf16[1040,256]{1,0:T(8,128)(2,1)S(1)} collective-permute-done((bf16[1040,256]{1,0:T(8,128)(2,1)S(1)}, bf16[1040,256]{1,0:T(8,128)(2,1)S(1)}, u32[]{:S(2)}, u32[]{:S(2)}) %collective-permute-start.5) | collective-permute-done | bytes 532512 | tf_op jit(solution)/shard_map/ppermute | solution.py:315
  38.4 2.3 %finish_one.1 = (bf16[4,128,256]{2,1,0:T(8,128)(2,1)S(1)}, f32[1,128,1024]{2,1,0:T(8,128)S(1)}) custom-call(s32[16]{0:T(128)S(1)} %copy-done.2, bf16[1040,256]{1,0:T(8,128)(2,1)S(1)} %collective-permute-done.5.piece2, bf16[4,128,256]{2,1,0:T(8,128)(2,1)S(1)} %collective-permute-done.7.kv, f32[4,128,256]{2,1,0:T(8,128)S(1)} %get-tuple-element.70.one_in), custom_call_target="tpu_custom_call" | custom-call | flops 20000000000 | bytes 20000000000 | tf_op jit(solution)/shard_map/finish_one/pallas_call | solution.py:375
  40.7 3.2 %collective-permute-start.11 = (bf16[4,128,256]{2,1,0:T(8,128)(2,1)S(1)}, bf16[4,128,256]{2,1,0:T(8,128)(2,1)S(1)}, u32[]{:S(2)}, u32[]{:S(2)}) collective-permute-start(bf16[4,128,256]{2,1,0:T(8,128)(2,1)S(1)} %get-tuple-element.79), channel_id=1, source_target_pairs={{0,252},{1,253},{2,254},{3,255},{4,0},{5,1},{6,2},{7,3},{8,4},{9,5... | collective-permute-start | bytes 786440 | tf_op jit(solution)/shard_map/ppermute | solution.py:319
  43.8 0.0 collective-permute-done.6.kv
  43.8 0.9 %all_two.1 = (bf16[3,128,256]{2,1,0:T(8,128)(2,1)S(1)}, f32[4,128,1024]{2,1,0:T(8,128)S(1)}, f32[1,128,1024]{2,1,0:T(8,128)S(1)}) custom-call(s32[16]{0:T(128)S(1)} %copy-done.2, bf16[1040,256]{1,0:T(8,128)(2,1)S(1)} %get-tuple-element.63.piece0, bf16[1040,256]{1,0:T(8,128)(2,1)S(1)} %collective-permute-done.3.piece1, ...), custom_call_target="tpu_custom_call" | custom-call | flops 20000000000 | bytes 20000000000 | tf_op jit(solution)/shard_map/all_two/pallas_call | solution.py:383
  44.7 0.1 collective-permute-start.12
  44.8 3.1 %finish_own.1 = (f32[4,128,256]{2,1,0:T(8,128)S(1)}, bf16[128,1024]{1,0:T(8,128)(2,1)S(1)}, bf16[128,1024]{1,0:T(8,128)(2,1)S(1)}, bf16[128,1024]{1,0:T(8,128)(2,1)S(1)}, bf16[128,1024]{1,0:T(8,128)(2,1)S(1)}) custom-call(s32[16]{0:T(128)S(1)} %copy-done.2, bf16[1040,256]{1,0:T(8,128)(2,1)S(1)} %collective-permute-done.5.piece2, ...), custom_call_target="tpu_custom_call" | custom-call | tf_op jit(solution)/shard_map/finish_own/pallas_call | solution.py:393
  47.9 3.9 %collective-permute-start.8 = (bf16[128,1024]{1,0:T(8,128)(2,1)S(1)}, bf16[128,1024]{1,0:T(8,128)(2,1)S(1)}, u32[]{:S(2)}, u32[]{:S(2)}) collective-permute-start(bf16[128,1024]{1,0:T(8,128)(2,1)S(1)} %get-tuple-element.75), channel_id=1, source_target_pairs={{0,3},{1,0},{2,1},{3,2},{4,7},{5,4},{6,5},{7,6},{8,11},{9,8},{10,9... | collective-permute-start | bytes 786440 | tf_op jit(solution)/shard_map/ppermute | solution.py:315
  51.8 0.0 collective-permute-start.9
  51.8 1.0 %collective-permute-start.10 = (bf16[128,1024]{1,0:T(8,128)(2,1)S(1)}, bf16[128,1024]{1,0:T(8,128)(2,1)S(1)}, u32[]{:S(2)}, u32[]{:S(2)}) collective-permute-start(bf16[128,1024]{1,0:T(8,128)(2,1)S(1)} %get-tuple-element.77), channel_id=1, source_target_pairs={{0,1},{1,2},{2,3},{3,0},{4,5},{5,6},{6,7},{7,4},{8,9},{9,10},{10,1... | collective-permute-start | bytes 786440 | tf_op jit(solution)/shard_map/ppermute | solution.py:315
  52.8 12.7 %collective-permute-done.12.two = bf16[3,128,256]{2,1,0:T(8,128)(2,1)S(1)} collective-permute-done((bf16[3,128,256]{2,1,0:T(8,128)(2,1)S(1)}, bf16[3,128,256]{2,1,0:T(8,128)(2,1)S(1)}, u32[]{:S(2)}, u32[]{:S(2)}) %collective-permute-start.12) | collective-permute-done | bytes 196640 | tf_op jit(solution)/shard_map/ppermute | solution.py:319
  65.5 0.0 collective-permute-done.11.one
  65.5 0.1 add_up.1
  65.6 2.1 %collective-permute-start.13 = (bf16[128,256]{1,0:T(8,128)(2,1)S(1)}, bf16[128,256]{1,0:T(8,128)(2,1)S(1)}, u32[]{:S(2)}, u32[]{:S(2)}) collective-permute-start(bf16[128,256]{1,0:T(8,128)(2,1)S(1)} %get-tuple-element.82), channel_id=1, source_target_pairs={{0,3},{1,0},{2,1},{3,2},{4,7},{5,4},{6,5},{7,6},{8,11},{9,8},{10,9... | collective-permute-start | bytes 196616 | tf_op jit(solution)/shard_map/ppermute | solution.py:315
  67.7 0.0 collective-permute-start.14
  67.7 0.0 collective-permute-done.8.piece1
  67.7 1.0 %collective-permute-start.15 = (bf16[128,256]{1,0:T(8,128)(2,1)S(1)}, bf16[128,256]{1,0:T(8,128)(2,1)S(1)}, u32[]{:S(2)}, u32[]{:S(2)}) collective-permute-start(bf16[128,256]{1,0:T(8,128)(2,1)S(1)} %get-tuple-element.84), channel_id=1, source_target_pairs={{0,1},{1,2},{2,3},{3,0},{4,5},{5,6},{6,7},{7,4},{8,9},{9,10},{10,1... | collective-permute-start | bytes 196616 | tf_op jit(solution)/shard_map/ppermute | solution.py:315
  68.6 0.0 collective-permute-done.9.piece2
  68.6 0.0 collective-permute-done.10.piece3
  68.6 1.0 %join_queries.1 = bf16[128,4096]{1,0:T(8,128)(2,1)} custom-call(bf16[128,1024]{1,0:T(8,128)(2,1)S(1)} %get-tuple-element.74.piece0, bf16[128,1024]{1,0:T(8,128)(2,1)S(1)} %collective-permute-done.8.piece1, bf16[128,1024]{1,0:T(8,128)(2,1)S(1)} %collective-permute-done.9.piece2, bf16[128,1024]{1,0:T(8,128)(2,1)S(1)} %collective-permute-done.10.piece3), custom_call_target="tpu_custom_call" | custom-call | tf_op jit(solution)/shard_map/join_queries/pallas_call | solution.py:402
  69.6 0.5 collective-permute-done.13.piece1
  70.2 3.4 %collective-permute-done.14.piece2 = bf16[128,256]{1,0:T(8,128)(2,1)S(1)} collective-permute-done((bf16[128,256]{1,0:T(8,128)(2,1)S(1)}, bf16[128,256]{1,0:T(8,128)(2,1)S(1)}, u32[]{:S(2)}, u32[]{:S(2)}) %collective-permute-start.14) | collective-permute-done | bytes 65568 | tf_op jit(solution)/shard_map/ppermute | solution.py:315
  73.5 0.3 collective-permute-done.15.piece3
  73.8 0.8 %join_kv.1 = (bf16[128,512]{1,0:T(8,128)(2,1)}, bf16[128,512]{1,0:T(8,128)(2,1)}) custom-call(bf16[128,256]{1,0:T(8,128)(2,1)S(1)} %get-tuple-element.81.piece0, bf16[128,256]{1,0:T(8,128)(2,1)S(1)} %collective-permute-done.13.piece1, bf16[128,256]{1,0:T(8,128)(2,1)S(1)} %collective-permute-done.14.piece2, bf16[128,256]{1,0:T(8,128)(2,1)S(1)} %collective-permute-done.15.piece3), custom_call_target="tpu_custom_call" | custom-call | tf_op jit(solution)/shard_map/join_kv/pallas_call | solution.py:416
  (2 shorter events, 0.0 us)
Async XLA Ops:
  2.3 12.3 %copy-start = (bf16[128,256]{1,0:T(8,128)(2,1)S(1)}, bf16[128,256]{1,0:T(8,128)(2,1)}, u32[]{:S(2)}) copy-start(bf16[128,256]{1,0:T(8,128)(2,1)} %get-tuple-element.54.piece0) | copy-start | bytes 196612
  2.3 8.6 %collective-permute-start = (bf16[128,256]{1,0:T(8,128)(2,1)}, bf16[128,256]{1,0:T(8,128)(2,1)S(1)}, u32[]{:S(2)}, u32[]{:S(2)}) collective-permute-start(bf16[128,256]{1,0:T(8,128)(2,1)} %get-tuple-element.46), channel_id=1, source_target_pairs={{0,1},{1,2},{2,3},{3,0},{4,5},{5,6},{6,7},{7,4},{8,9},{9,10},{10,1... | collective-permute-start | bytes 196616 | tf_op jit(solution)/shard_map/ppermute | solution.py:315
  3.9 6.9 %collective-permute-start.1 = (bf16[128,256]{1,0:T(8,128)(2,1)}, bf16[128,256]{1,0:T(8,128)(2,1)S(1)}, u32[]{:S(2)}, u32[]{:S(2)}) collective-permute-start(bf16[128,256]{1,0:T(8,128)(2,1)} %get-tuple-element.47), channel_id=1, source_target_pairs={{0,2},{1,3},{2,0},{3,1},{4,6},{5,7},{6,4},{7,5},{8,10},{9,11},{10,... | collective-permute-start | bytes 196616 | tf_op jit(solution)/shard_map/ppermute | solution.py:315
  6.8 4.5 %collective-permute-start.2 = (bf16[128,256]{1,0:T(8,128)(2,1)}, bf16[128,256]{1,0:T(8,128)(2,1)S(1)}, u32[]{:S(2)}, u32[]{:S(2)}) collective-permute-start(bf16[128,256]{1,0:T(8,128)(2,1)} %get-tuple-element.48), channel_id=1, source_target_pairs={{0,3},{1,0},{2,1},{3,2},{4,7},{5,4},{6,5},{7,6},{8,11},{9,8},{10,9... | collective-permute-start | bytes 196616 | tf_op jit(solution)/shard_map/ppermute | solution.py:315
  8.2 0.7 copy-start.1
  10.9 16.4 %copy-start.2 = (s32[16]{0:T(128)S(1)}, s32[16]{0:T(128)}, u32[]{:S(2)}) copy-start(s32[16]{0:T(128)} %doc_start.9) | copy-start | bytes 196
  11.3 13.9 %collective-permute-start.3 = (bf16[1040,256]{1,0:T(8,128)(2,1)S(1)}, bf16[1040,256]{1,0:T(8,128)(2,1)S(1)}, u32[]{:S(2)}, u32[]{:S(2)}) collective-permute-start(bf16[1040,256]{1,0:T(8,128)(2,1)S(1)} %get-tuple-element.52), channel_id=1, source_target_pairs={{0,1},{1,2},{2,3},{3,0},{4,5},{5,6},{6,7},{7,4},{8,9},{9,10},{10,1... | collective-permute-start | bytes 1597448 | tf_op jit(solution)/shard_map/ppermute | solution.py:315
  11.7 13.5 %collective-permute-start.4 = (bf16[1040,256]{1,0:T(8,128)(2,1)S(1)}, bf16[1040,256]{1,0:T(8,128)(2,1)S(1)}, u32[]{:S(2)}, u32[]{:S(2)}) collective-permute-start(bf16[1040,256]{1,0:T(8,128)(2,1)S(1)} %get-tuple-element.53), channel_id=1, source_target_pairs={{0,3},{1,0},{2,1},{3,2},{4,7},{5,4},{6,5},{7,6},{8,11},{9,8},{10,9... | collective-permute-start | bytes 1597448 | tf_op jit(solution)/shard_map/ppermute | solution.py:315
  14.6 17.7 %collective-permute-start.7 = (bf16[4,128,256]{2,1,0:T(8,128)(2,1)S(1)}, bf16[4,128,256]{2,1,0:T(8,128)(2,1)S(1)}, u32[]{:S(2)}, u32[]{:S(2)}) collective-permute-start(bf16[4,128,256]{2,1,0:T(8,128)(2,1)S(1)} %get-tuple-element.62.kv), channel_id=1, source_target_pairs={{0,4},{1,5},{2,6},{3,7},{4,8},{5,9},{6,10},{7,11},{8,12},{9,13},{1... | collective-permute-start | bytes 786440 | tf_op jit(solution)/shard_map/ppermute | solution.py:319
  18.0 25.9 %collective-permute-start.6 = (bf16[3,128,256]{2,1,0:T(8,128)(2,1)S(1)}, bf16[3,128,256]{2,1,0:T(8,128)(2,1)S(1)}, u32[]{:S(2)}, u32[]{:S(2)}) collective-permute-start(bf16[3,128,256]{2,1,0:T(8,128)(2,1)S(1)} %get-tuple-element.67), channel_id=1, source_target_pairs={{0,8},{1,9},{2,10},{3,11},{4,12},{5,13},{6,14},{7,15},{8,16},{9,17... | collective-permute-start | bytes 589832 | tf_op jit(solution)/shard_map/ppermute | solution.py:319
  25.2 13.2 %collective-permute-start.5 = (bf16[1040,256]{1,0:T(8,128)(2,1)S(1)}, bf16[1040,256]{1,0:T(8,128)(2,1)S(1)}, u32[]{:S(2)}, u32[]{:S(2)}) collective-permute-start(bf16[1040,256]{1,0:T(8,128)(2,1)S(1)} %get-tuple-element.61), channel_id=1, source_target_pairs={{0,2},{1,3},{2,0},{3,1},{4,6},{5,7},{6,4},{7,5},{8,10},{9,11},{10,... | collective-permute-start | bytes 1597448 | tf_op jit(solution)/shard_map/ppermute | solution.py:315
  40.7 24.8 %collective-permute-start.11 = (bf16[4,128,256]{2,1,0:T(8,128)(2,1)S(1)}, bf16[4,128,256]{2,1,0:T(8,128)(2,1)S(1)}, u32[]{:S(2)}, u32[]{:S(2)}) collective-permute-start(bf16[4,128,256]{2,1,0:T(8,128)(2,1)S(1)} %get-tuple-element.79), channel_id=1, source_target_pairs={{0,252},{1,253},{2,254},{3,255},{4,0},{5,1},{6,2},{7,3},{8,4},{9,5... | collective-permute-start | bytes 786440 | tf_op jit(solution)/shard_map/ppermute | solution.py:319
  44.7 20.8 %collective-permute-start.12 = (bf16[3,128,256]{2,1,0:T(8,128)(2,1)S(1)}, bf16[3,128,256]{2,1,0:T(8,128)(2,1)S(1)}, u32[]{:S(2)}, u32[]{:S(2)}) collective-permute-start(bf16[3,128,256]{2,1,0:T(8,128)(2,1)S(1)} %get-tuple-element.80), channel_id=1, source_target_pairs={{0,248},{1,249},{2,250},{3,251},{4,252},{5,253},{6,254},{7,255},{8... | collective-permute-start | bytes 589832 | tf_op jit(solution)/shard_map/ppermute | solution.py:319
  47.9 19.8 %collective-permute-start.8 = (bf16[128,1024]{1,0:T(8,128)(2,1)S(1)}, bf16[128,1024]{1,0:T(8,128)(2,1)S(1)}, u32[]{:S(2)}, u32[]{:S(2)}) collective-permute-start(bf16[128,1024]{1,0:T(8,128)(2,1)S(1)} %get-tuple-element.75), channel_id=1, source_target_pairs={{0,3},{1,0},{2,1},{3,2},{4,7},{5,4},{6,5},{7,6},{8,11},{9,8},{10,9... | collective-permute-start | bytes 786440 | tf_op jit(solution)/shard_map/ppermute | solution.py:315
  51.8 16.8 %collective-permute-start.9 = (bf16[128,1024]{1,0:T(8,128)(2,1)S(1)}, bf16[128,1024]{1,0:T(8,128)(2,1)S(1)}, u32[]{:S(2)}, u32[]{:S(2)}) collective-permute-start(bf16[128,1024]{1,0:T(8,128)(2,1)S(1)} %get-tuple-element.76), channel_id=1, source_target_pairs={{0,2},{1,3},{2,0},{3,1},{4,6},{5,7},{6,4},{7,5},{8,10},{9,11},{10,... | collective-permute-start | bytes 786440 | tf_op jit(solution)/shard_map/ppermute | solution.py:315
  51.8 16.8 %collective-permute-start.10 = (bf16[128,1024]{1,0:T(8,128)(2,1)S(1)}, bf16[128,1024]{1,0:T(8,128)(2,1)S(1)}, u32[]{:S(2)}, u32[]{:S(2)}) collective-permute-start(bf16[128,1024]{1,0:T(8,128)(2,1)S(1)} %get-tuple-element.77), channel_id=1, source_target_pairs={{0,1},{1,2},{2,3},{3,0},{4,5},{5,6},{6,7},{7,4},{8,9},{9,10},{10,1... | collective-permute-start | bytes 786440 | tf_op jit(solution)/shard_map/ppermute | solution.py:315
  65.6 4.6 %collective-permute-start.13 = (bf16[128,256]{1,0:T(8,128)(2,1)S(1)}, bf16[128,256]{1,0:T(8,128)(2,1)S(1)}, u32[]{:S(2)}, u32[]{:S(2)}) collective-permute-start(bf16[128,256]{1,0:T(8,128)(2,1)S(1)} %get-tuple-element.82), channel_id=1, source_target_pairs={{0,3},{1,0},{2,1},{3,2},{4,7},{5,4},{6,5},{7,6},{8,11},{9,8},{10,9... | collective-permute-start | bytes 196616 | tf_op jit(solution)/shard_map/ppermute | solution.py:315
  67.7 5.9 %collective-permute-start.14 = (bf16[128,256]{1,0:T(8,128)(2,1)S(1)}, bf16[128,256]{1,0:T(8,128)(2,1)S(1)}, u32[]{:S(2)}, u32[]{:S(2)}) collective-permute-start(bf16[128,256]{1,0:T(8,128)(2,1)S(1)} %get-tuple-element.83), channel_id=1, source_target_pairs={{0,2},{1,3},{2,0},{3,1},{4,6},{5,7},{6,4},{7,5},{8,10},{9,11},{10,... | collective-permute-start | bytes 196616 | tf_op jit(solution)/shard_map/ppermute | solution.py:315
  67.7 6.2 %collective-permute-start.15 = (bf16[128,256]{1,0:T(8,128)(2,1)S(1)}, bf16[128,256]{1,0:T(8,128)(2,1)S(1)}, u32[]{:S(2)}, u32[]{:S(2)}) collective-permute-start(bf16[128,256]{1,0:T(8,128)(2,1)S(1)} %get-tuple-element.84), channel_id=1, source_target_pairs={{0,1},{1,2},{2,3},{3,0},{4,5},{5,6},{6,7},{7,4},{8,9},{9,10},{10,1... | collective-permute-start | bytes 196616 | tf_op jit(solution)/shard_map/ppermute | solution.py:315

commit v2 on v1

--- a/solution.py
+++ b/solution.py
@@ -158,7 +158,28 @@
         query_place = lax.rem(place + ROW - slot, ROW)
         start = doc_start[own_row * ROW + query_place]
 
-        def turn(key_slot, carry, slot=slot, piece=piece, start=start, query_place=query_place):
+        def work(key_slot, count, slot=slot, piece=piece, query_place=query_place):
+            keys = count * BLOCK
+            span = pl.ds(key_slot, count)
+            key = kv[span, :, :DH].reshape(keys, DH)
+            value = kv[span, :, DH:].reshape(keys, DH)
+            query = stacked(piece, 0)
+            grad = stacked(piece, HALF)
+            stats = piece[STAT:, :].astype(F32)
+            norm = side_by_side(stats[0:4])
+            dots = side_by_side(stats[4:8] + stats[8:12] + stats[12:16])
+            weights = jnp.exp(nt(key, query) * SCALE - norm)
+            if back == 0:
+                key_pos = lax.broadcasted_iota(jnp.int32, (BLOCK, WIDE), 0)
+                query_pos = lax.broadcasted_iota(jnp.int32, (BLOCK, WIDE), 1) % BLOCK
+                ahead = (query_place - key_slot) * BLOCK
+                weights = jnp.where(key_pos <= query_pos + ahead, weights, 0.0)
+            grad_scores = (weights * (nt(value, grad) - dots)).astype(BF16)
+            dkv[span, :, DH:] += nn(weights.astype(BF16), grad).reshape(count, BLOCK, DH)
+            dkv[span, :, :DH] += nn(grad_scores, query).reshape(count, BLOCK, DH)
+            dq[slot] += nn(key.T, grad_scores)
+
+        def turn(key_slot, carry, start=start, query_place=query_place, work=work):
             key_place = key_slot + (1 if back == 2 else 0)
             seen = first_key + key_place >= start
             if back == 0:
@@ -166,27 +187,22 @@
 
             @pl.when(seen)
             def _():
-                key = kv[key_slot, :, :DH]
-                value = kv[key_slot, :, DH:]
-                query = stacked(piece, 0)
-                grad = stacked(piece, HALF)
-                stats = piece[STAT:, :].astype(F32)
-                norm = side_by_side(stats[0:4])
-                dots = side_by_side(stats[4:8] + stats[8:12] + stats[12:16])
-                weights = jnp.exp(nt(key, query) * SCALE - norm)
-                if back == 0:
-                    key_pos = lax.broadcasted_iota(jnp.int32, (BLOCK, WIDE), 0)
-                    query_pos = lax.broadcasted_iota(jnp.int32, (BLOCK, WIDE), 1) % BLOCK
-                    ahead = (query_place - key_place) * BLOCK
-                    weights = jnp.where(key_pos <= query_pos + ahead, weights, 0.0)
-                grad_scores = (weights * (nt(value, grad) - dots)).astype(BF16)
-                dkv[key_slot, :, DH:] += nn(weights.astype(BF16), grad)
-                dkv[key_slot, :, :DH] += nn(grad_scores, query)
-                dq[slot] += nn(key.T, grad_scores)
+                work(key_slot, 1)
 
             return carry
 
-        lax.fori_loop(0, ROW - 1 if back == 2 else ROW, turn, 0)
+        if back == 1:
+            whole = first_key >= start
+
+            @pl.when(whole)
+            def _(work=work):
+                work(0, ROW)
+
+            @pl.when(jnp.logical_not(whole))
+            def _(turn=turn):
+                lax.fori_loop(1, ROW, turn, 0)
+        else:
+            lax.fori_loop(0, ROW - 1 if back == 2 else ROW, turn, 0)
 
 
 def begin_own(doc_start, piece0, piece1, piece3, kv, dkv, dq):

time: 75.6 us -> 75.4 us (level)
  the two profiles are of different devices: /device:TPU:32 before, /device:TPU:38 now
where the time goes in v2:
time: 75.4 us; the launch traced here: 74.7 us
  starting transfers between devices  28.1 us (37%)
  waiting for transfers between devices  27 us (36%)
  Pallas kernels  17.9 us (24%)
  between operations  0.96 us (1%)
    ppermute x4, waiting for transfers between devices, along_rows(): lax.ppermute(value, AXES, [(b, (b + by) % total) for b in range(total)])  22.7 us
    ppermute x12, starting transfers between devices, along_row(): return lax.ppermute(value, AXES, pairs)  16.7 us
    ppermute x4, starting transfers between devices, along_rows(): lax.ppermute(value, AXES, [(b, (b + by) % total) for b in range(total)])  11.4 us
    ppermute x12, waiting for transfers between devices, along_row(): return lax.ppermute(value, AXES, pairs)  4.35 us
    pallas_call x1, Pallas kernels, per_device(): kernel(begin_own, 'begin_own', [SMEM] + [VMEM] * 4, [(kv_shape, F32), dq_...  3.25 us
    pallas_call x1, Pallas kernels, per_device(): kernel(finish_own, 'finish_own', [SMEM] + [VMEM] * 5, [(kv_shape, F32)] +...  3.08 us
    pallas_call x1, Pallas kernels, per_device(): kernel(begin_one, 'begin_one', [SMEM] + [VMEM] * 5, [(kv_shape, F32), dq_...  2.02 us
    pallas_call x1, Pallas kernels, per_device(): kernel(functools.partial(pack, (1, 3)), 'pack_near', [HBM] * 4, [piece_sh...  1.95 us
  transfers between devices with their start and end apart: 16, of which 6 were waited for; matrix products, arithmetic and copies ran while one was open for 0% of the time, Pallas kernels for 21%

profile of v2, /device:TPU:38, one launch (start us, length us, event | category | flops | bytes accessed | tf_op | source)
XLA Modules:
  0.0 74.7 jit_solution(17915495017395103425)
XLA Ops:
  0.6 1.6 %pack_kv.1 = (bf16[128,256]{1,0:T(8,128)(2,1)}, bf16[128,256]{1,0:T(8,128)(2,1)}, bf16[128,256]{1,0:T(8,128)(2,1)}, bf16[128,256]{1,0:T(8,128)(2,1)}) custom-call(bf16[128,512]{1,0:T(8,128)(2,1)} %keys.1, bf16[128,512]{1,0:T(8,128)(2,1)} %values.1), custom_call_target="tpu_custom_call" | custom-call | tf_op jit(solution)/shard_map/pack_kv/pallas_call | solution.py:351
  2.3 0.0 copy-start
  2.3 1.7 %collective-permute-start = (bf16[128,256]{1,0:T(8,128)(2,1)}, bf16[128,256]{1,0:T(8,128)(2,1)S(1)}, u32[]{:S(2)}, u32[]{:S(2)}) collective-permute-start(bf16[128,256]{1,0:T(8,128)(2,1)} %get-tuple-element.46), channel_id=1, source_target_pairs={{0,1},{1,2},{2,3},{3,0},{4,5},{5,6},{6,7},{7,4},{8,9},{9,10},{10,1... | collective-permute-start | bytes 196616 | tf_op jit(solution)/shard_map/ppermute | solution.py:331
  3.9 2.9 %collective-permute-start.1 = (bf16[128,256]{1,0:T(8,128)(2,1)}, bf16[128,256]{1,0:T(8,128)(2,1)S(1)}, u32[]{:S(2)}, u32[]{:S(2)}) collective-permute-start(bf16[128,256]{1,0:T(8,128)(2,1)} %get-tuple-element.47), channel_id=1, source_target_pairs={{0,2},{1,3},{2,0},{3,1},{4,6},{5,7},{6,4},{7,5},{8,10},{9,11},{10,... | collective-permute-start | bytes 196616 | tf_op jit(solution)/shard_map/ppermute | solution.py:331
  6.8 1.3 %collective-permute-start.2 = (bf16[128,256]{1,0:T(8,128)(2,1)}, bf16[128,256]{1,0:T(8,128)(2,1)S(1)}, u32[]{:S(2)}, u32[]{:S(2)}) collective-permute-start(bf16[128,256]{1,0:T(8,128)(2,1)} %get-tuple-element.48), channel_id=1, source_target_pairs={{0,3},{1,0},{2,1},{3,2},{4,7},{5,4},{6,5},{7,6},{8,11},{9,8},{10,9... | collective-permute-start | bytes 196616 | tf_op jit(solution)/shard_map/ppermute | solution.py:331
  8.2 0.7 copy-done.1
  8.9 2.0 %pack_near.1 = (bf16[1040,256]{1,0:T(8,128)(2,1)S(1)}, bf16[1040,256]{1,0:T(8,128)(2,1)S(1)}) custom-call(bf16[128,4096]{1,0:T(8,128)(2,1)} %queries.3, bf16[128,4096]{1,0:T(8,128)(2,1)} %outputs.3, bf16[128,4096]{1,0:T(8,128)(2,1)} %grads.1, bf16[32,128]{1,0:T(8,128)(2,1)S(1)} %bitcast.1), custom_call_target="tpu_custom_call" | custom-call | tf_op jit(solution)/shard_map/pack_near/pallas_call | solution.py:356
  10.9 0.0 copy-start.2
  10.9 0.0 collective-permute-done.piece1
  10.9 0.0 collective-permute-done.1.piece2
  10.9 0.4 collective-permute-done.2.piece3
  11.3 0.3 collective-permute-start.3
  11.7 2.9 %collective-permute-start.4 = (bf16[1040,256]{1,0:T(8,128)(2,1)S(1)}, bf16[1040,256]{1,0:T(8,128)(2,1)S(1)}, u32[]{:S(2)}, u32[]{:S(2)}) collective-permute-start(bf16[1040,256]{1,0:T(8,128)(2,1)S(1)} %get-tuple-element.53), channel_id=1, source_target_pairs={{0,3},{1,0},{2,1},{3,2},{4,7},{5,4},{6,5},{7,6},{8,11},{9,8},{10,9... | collective-permute-start | bytes 1597448 | tf_op jit(solution)/shard_map/ppermute | solution.py:331
  14.6 0.0 copy-done
  14.6 3.3 %collective-permute-start.7 = (bf16[4,128,256]{2,1,0:T(8,128)(2,1)S(1)}, bf16[4,128,256]{2,1,0:T(8,128)(2,1)S(1)}, u32[]{:S(2)}, u32[]{:S(2)}) collective-permute-start(bf16[4,128,256]{2,1,0:T(8,128)(2,1)S(1)} %get-tuple-element.62.kv), channel_id=1, source_target_pairs={{0,4},{1,5},{2,6},{3,7},{4,8},{5,9},{6,10},{7,11},{8,12},{9,13},{1... | collective-permute-start | bytes 786440 | tf_op jit(solution)/shard_map/ppermute | solution.py:335
  18.0 4.5 %collective-permute-start.6 = (bf16[3,128,256]{2,1,0:T(8,128)(2,1)S(1)}, bf16[3,128,256]{2,1,0:T(8,128)(2,1)S(1)}, u32[]{:S(2)}, u32[]{:S(2)}) collective-permute-start(bf16[3,128,256]{2,1,0:T(8,128)(2,1)S(1)} %get-tuple-element.67), channel_id=1, source_target_pairs={{0,8},{1,9},{2,10},{3,11},{4,12},{5,13},{6,14},{7,15},{8,16},{9,17... | collective-permute-start | bytes 589832 | tf_op jit(solution)/shard_map/ppermute | solution.py:335
  22.5 2.0 %pack_rest.1 = (bf16[1040,256]{1,0:T(8,128)(2,1)S(1)}, bf16[1040,256]{1,0:T(8,128)(2,1)S(1)}) custom-call(bf16[128,4096]{1,0:T(8,128)(2,1)} %queries.3, bf16[128,4096]{1,0:T(8,128)(2,1)} %outputs.3, bf16[128,4096]{1,0:T(8,128)(2,1)} %grads.1, bf16[32,128]{1,0:T(8,128)(2,1)S(1)} %bitcast.2), custom_call_target="tpu_custom_call" | custom-call | tf_op jit(solution)/shard_map/pack_rest/pallas_call | solution.py:373
  24.4 0.8 %collective-permute-done.3.piece1 = bf16[1040,256]{1,0:T(8,128)(2,1)S(1)} collective-permute-done((bf16[1040,256]{1,0:T(8,128)(2,1)S(1)}, bf16[1040,256]{1,0:T(8,128)(2,1)S(1)}, u32[]{:S(2)}, u32[]{:S(2)}) %collective-permute-start.3) | collective-permute-done | bytes 532512 | tf_op jit(solution)/shard_map/ppermute | solution.py:331
  25.2 0.0 collective-permute-done.4.piece3
  25.2 2.1 %collective-permute-start.5 = (bf16[1040,256]{1,0:T(8,128)(2,1)S(1)}, bf16[1040,256]{1,0:T(8,128)(2,1)S(1)}, u32[]{:S(2)}, u32[]{:S(2)}) collective-permute-start(bf16[1040,256]{1,0:T(8,128)(2,1)S(1)} %get-tuple-element.61), channel_id=1, source_target_pairs={{0,2},{1,3},{2,0},{3,1},{4,6},{5,7},{6,4},{7,5},{8,10},{9,11},{10,... | collective-permute-start | bytes 1597448 | tf_op jit(solution)/shard_map/ppermute | solution.py:331
  27.3 0.0 copy-done.2
  27.3 3.2 %begin_own.1 = (f32[4,128,256]{2,1,0:T(8,128)S(1)}, f32[4,128,1024]{2,1,0:T(8,128)S(1)}) custom-call(s32[16]{0:T(128)S(1)} %copy-done.2, bf16[1040,256]{1,0:T(8,128)(2,1)S(1)} %get-tuple-element.63.piece0, bf16[1040,256]{1,0:T(8,128)(2,1)S(1)} %collective-permute-done.3.piece1, bf16[1040,256]{1,0:T(8,128)(2,1)S(1)} %collective-permute-done.4.piece3, ...), custom_call_target="tpu_custom_call" | custom-call | flops 20000000000 | bytes 20000000000 | tf_op jit(solution)/shard_map/begin_own/pallas_call | solution.py:384
  30.6 6.6 %collective-permute-done.7.kv = bf16[4,128,256]{2,1,0:T(8,128)(2,1)S(1)} collective-permute-done((bf16[4,128,256]{2,1,0:T(8,128)(2,1)S(1)}, bf16[4,128,256]{2,1,0:T(8,128)(2,1)S(1)}, u32[]{:S(2)}, u32[]{:S(2)}) %collective-permute-start.7) | collective-permute-done | bytes 262176 | tf_op jit(solution)/shard_map/ppermute | solution.py:335
  37.2 2.0 %begin_one.1 = (f32[4,128,256]{2,1,0:T(8,128)S(1)}, f32[4,128,1024]{2,1,0:T(8,128)S(1)}) custom-call(s32[16]{0:T(128)S(1)} %copy-done.2, bf16[1040,256]{1,0:T(8,128)(2,1)S(1)} %get-tuple-element.63.piece0, bf16[1040,256]{1,0:T(8,128)(2,1)S(1)} %collective-permute-done.3.piece1, bf16[1040,256]{1,0:T(8,128)(2,1)S(1)} %collective-permute-done.4.piece3, ...), custom_call_target="tpu_custom_call" | custom-call | flops 20000000000 | bytes 20000000000 | tf_op jit(solution)/shard_map/begin_one/pallas_call | solution.py:387
  39.2 0.0 collective-permute-done.5.piece2
  39.2 1.2 %finish_one.1 = (bf16[4,128,256]{2,1,0:T(8,128)(2,1)S(1)}, f32[1,128,1024]{2,1,0:T(8,128)S(1)}) custom-call(s32[16]{0:T(128)S(1)} %copy-done.2, bf16[1040,256]{1,0:T(8,128)(2,1)S(1)} %collective-permute-done.5.piece2, bf16[4,128,256]{2,1,0:T(8,128)(2,1)S(1)} %collective-permute-done.7.kv, f32[4,128,256]{2,1,0:T(8,128)S(1)} %get-tuple-element.70.one_in), custom_call_target="tpu_custom_call" | custom-call | flops 20000000000 | bytes 20000000000 | tf_op jit(solution)/shard_map/finish_one/pallas_call | solution.py:391
  40.4 0.8 %collective-permute-start.11 = (bf16[4,128,256]{2,1,0:T(8,128)(2,1)S(1)}, bf16[4,128,256]{2,1,0:T(8,128)(2,1)S(1)}, u32[]{:S(2)}, u32[]{:S(2)}) collective-permute-start(bf16[4,128,256]{2,1,0:T(8,128)(2,1)S(1)} %get-tuple-element.79), channel_id=1, source_target_pairs={{0,252},{1,253},{2,254},{3,255},{4,0},{5,1},{6,2},{7,3},{8,4},{9,5... | collective-permute-start | bytes 786440 | tf_op jit(solution)/shard_map/ppermute | solution.py:335
  41.3 0.0 collective-permute-done.6.kv
  41.3 0.9 %all_two.1 = (bf16[3,128,256]{2,1,0:T(8,128)(2,1)S(1)}, f32[4,128,1024]{2,1,0:T(8,128)S(1)}, f32[1,128,1024]{2,1,0:T(8,128)S(1)}) custom-call(s32[16]{0:T(128)S(1)} %copy-done.2, bf16[1040,256]{1,0:T(8,128)(2,1)S(1)} %get-tuple-element.63.piece0, bf16[1040,256]{1,0:T(8,128)(2,1)S(1)} %collective-permute-done.3.piece1, ...), custom_call_target="tpu_custom_call" | custom-call | flops 20000000000 | bytes 20000000000 | tf_op jit(solution)/shard_map/all_two/pallas_call | solution.py:399
  42.2 2.7 %collective-permute-start.12 = (bf16[3,128,256]{2,1,0:T(8,128)(2,1)S(1)}, bf16[3,128,256]{2,1,0:T(8,128)(2,1)S(1)}, u32[]{:S(2)}, u32[]{:S(2)}) collective-permute-start(bf16[3,128,256]{2,1,0:T(8,128)(2,1)S(1)} %get-tuple-element.80), channel_id=1, source_target_pairs={{0,248},{1,249},{2,250},{3,251},{4,252},{5,253},{6,254},{7,255},{8... | collective-permute-start | bytes 589832 | tf_op jit(solution)/shard_map/ppermute | solution.py:335
  44.8 3.1 %finish_own.1 = (f32[4,128,256]{2,1,0:T(8,128)S(1)}, bf16[128,1024]{1,0:T(8,128)(2,1)S(1)}, bf16[128,1024]{1,0:T(8,128)(2,1)S(1)}, bf16[128,1024]{1,0:T(8,128)(2,1)S(1)}, bf16[128,1024]{1,0:T(8,128)(2,1)S(1)}) custom-call(s32[16]{0:T(128)S(1)} %copy-done.2, bf16[1040,256]{1,0:T(8,128)(2,1)S(1)} %collective-permute-done.5.piece2, ...), custom_call_target="tpu_custom_call" | custom-call | tf_op jit(solution)/shard_map/finish_own/pallas_call | solution.py:409
  47.9 1.2 %collective-permute-start.8 = (bf16[128,1024]{1,0:T(8,128)(2,1)S(1)}, bf16[128,1024]{1,0:T(8,128)(2,1)S(1)}, u32[]{:S(2)}, u32[]{:S(2)}) collective-permute-start(bf16[128,1024]{1,0:T(8,128)(2,1)S(1)} %get-tuple-element.75), channel_id=1, source_target_pairs={{0,3},{1,0},{2,1},{3,2},{4,7},{5,4},{6,5},{7,6},{8,11},{9,8},{10,9... | collective-permute-start | bytes 786440 | tf_op jit(solution)/shard_map/ppermute | solution.py:331
  49.1 0.0 collective-permute-start.9
  49.1 1.0 %collective-permute-start.10 = (bf16[128,1024]{1,0:T(8,128)(2,1)S(1)}, bf16[128,1024]{1,0:T(8,128)(2,1)S(1)}, u32[]{:S(2)}, u32[]{:S(2)}) collective-permute-start(bf16[128,1024]{1,0:T(8,128)(2,1)S(1)} %get-tuple-element.77), channel_id=1, source_target_pairs={{0,1},{1,2},{2,3},{3,0},{4,5},{5,6},{6,7},{7,4},{8,9},{9,10},{10,1... | collective-permute-start | bytes 786440 | tf_op jit(solution)/shard_map/ppermute | solution.py:331
  50.1 16.0 %collective-permute-done.12.two = bf16[3,128,256]{2,1,0:T(8,128)(2,1)S(1)} collective-permute-done((bf16[3,128,256]{2,1,0:T(8,128)(2,1)S(1)}, bf16[3,128,256]{2,1,0:T(8,128)(2,1)S(1)}, u32[]{:S(2)}, u32[]{:S(2)}) %collective-permute-start.12) | collective-permute-done | bytes 196640 | tf_op jit(solution)/shard_map/ppermute | solution.py:335
  66.1 0.0 collective-permute-done.11.one
  66.1 0.1 add_up.1
  66.2 0.1 collective-permute-start.13
  66.3 1.9 %collective-permute-start.14 = (bf16[128,256]{1,0:T(8,128)(2,1)S(1)}, bf16[128,256]{1,0:T(8,128)(2,1)S(1)}, u32[]{:S(2)}, u32[]{:S(2)}) collective-permute-start(bf16[128,256]{1,0:T(8,128)(2,1)S(1)} %get-tuple-element.83), channel_id=1, source_target_pairs={{0,2},{1,3},{2,0},{3,1},{4,6},{5,7},{6,4},{7,5},{8,10},{9,11},{10,... | collective-permute-start | bytes 196616 | tf_op jit(solution)/shard_map/ppermute | solution.py:331
  68.2 0.0 collective-permute-done.8.piece1
  68.3 1.3 %collective-permute-start.15 = (bf16[128,256]{1,0:T(8,128)(2,1)S(1)}, bf16[128,256]{1,0:T(8,128)(2,1)S(1)}, u32[]{:S(2)}, u32[]{:S(2)}) collective-permute-start(bf16[128,256]{1,0:T(8,128)(2,1)S(1)} %get-tuple-element.84), channel_id=1, source_target_pairs={{0,1},{1,2},{2,3},{3,0},{4,5},{5,6},{6,7},{7,4},{8,9},{9,10},{10,1... | collective-permute-start | bytes 196616 | tf_op jit(solution)/shard_map/ppermute | solution.py:331
  69.6 0.0 collective-permute-done.9.piece2
  69.6 0.0 collective-permute-done.10.piece3
  69.6 1.0 %join_queries.1 = bf16[128,4096]{1,0:T(8,128)(2,1)} custom-call(bf16[128,1024]{1,0:T(8,128)(2,1)S(1)} %get-tuple-element.74.piece0, bf16[128,1024]{1,0:T(8,128)(2,1)S(1)} %collective-permute-done.8.piece1, bf16[128,1024]{1,0:T(8,128)(2,1)S(1)} %collective-permute-done.9.piece2, bf16[128,1024]{1,0:T(8,128)(2,1)S(1)} %collective-permute-done.10.piece3), custom_call_target="tpu_custom_call" | custom-call | tf_op jit(solution)/shard_map/join_queries/pallas_call | solution.py:418
  70.6 0.0 collective-permute-done.13.piece1
  70.6 1.7 %collective-permute-done.14.piece2 = bf16[128,256]{1,0:T(8,128)(2,1)S(1)} collective-permute-done((bf16[128,256]{1,0:T(8,128)(2,1)S(1)}, bf16[128,256]{1,0:T(8,128)(2,1)S(1)}, u32[]{:S(2)}, u32[]{:S(2)}) %collective-permute-start.14) | collective-permute-done | bytes 65568 | tf_op jit(solution)/shard_map/ppermute | solution.py:331
  72.3 1.4 %collective-permute-done.15.piece3 = bf16[128,256]{1,0:T(8,128)(2,1)S(1)} collective-permute-done((bf16[128,256]{1,0:T(8,128)(2,1)S(1)}, bf16[128,256]{1,0:T(8,128)(2,1)S(1)}, u32[]{:S(2)}, u32[]{:S(2)}) %collective-permute-start.15) | collective-permute-done | bytes 65568 | tf_op jit(solution)/shard_map/ppermute | solution.py:331
  73.7 0.8 %join_kv.1 = (bf16[128,512]{1,0:T(8,128)(2,1)}, bf16[128,512]{1,0:T(8,128)(2,1)}) custom-call(bf16[128,256]{1,0:T(8,128)(2,1)S(1)} %get-tuple-element.81.piece0, bf16[128,256]{1,0:T(8,128)(2,1)S(1)} %collective-permute-done.13.piece1, bf16[128,256]{1,0:T(8,128)(2,1)S(1)} %collective-permute-done.14.piece2, bf16[128,256]{1,0:T(8,128)(2,1)S(1)} %collective-permute-done.15.piece3), custom_call_target="tpu_custom_call" | custom-call | tf_op jit(solution)/shard_map/join_kv/pallas_call | solution.py:432
  (2 shorter events, 0.0 us)
Async XLA Ops:
  2.3 12.3 %copy-start = (bf16[128,256]{1,0:T(8,128)(2,1)S(1)}, bf16[128,256]{1,0:T(8,128)(2,1)}, u32[]{:S(2)}) copy-start(bf16[128,256]{1,0:T(8,128)(2,1)} %get-tuple-element.54.piece0) | copy-start | bytes 196612
  2.3 8.6 %collective-permute-start = (bf16[128,256]{1,0:T(8,128)(2,1)}, bf16[128,256]{1,0:T(8,128)(2,1)S(1)}, u32[]{:S(2)}, u32[]{:S(2)}) collective-permute-start(bf16[128,256]{1,0:T(8,128)(2,1)} %get-tuple-element.46), channel_id=1, source_target_pairs={{0,1},{1,2},{2,3},{3,0},{4,5},{5,6},{6,7},{7,4},{8,9},{9,10},{10,1... | collective-permute-start | bytes 196616 | tf_op jit(solution)/shard_map/ppermute | solution.py:331
  3.9 6.9 %collective-permute-start.1 = (bf16[128,256]{1,0:T(8,128)(2,1)}, bf16[128,256]{1,0:T(8,128)(2,1)S(1)}, u32[]{:S(2)}, u32[]{:S(2)}) collective-permute-start(bf16[128,256]{1,0:T(8,128)(2,1)} %get-tuple-element.47), channel_id=1, source_target_pairs={{0,2},{1,3},{2,0},{3,1},{4,6},{5,7},{6,4},{7,5},{8,10},{9,11},{10,... | collective-permute-start | bytes 196616 | tf_op jit(solution)/shard_map/ppermute | solution.py:331
  6.8 4.5 %collective-permute-start.2 = (bf16[128,256]{1,0:T(8,128)(2,1)}, bf16[128,256]{1,0:T(8,128)(2,1)S(1)}, u32[]{:S(2)}, u32[]{:S(2)}) collective-permute-start(bf16[128,256]{1,0:T(8,128)(2,1)} %get-tuple-element.48), channel_id=1, source_target_pairs={{0,3},{1,0},{2,1},{3,2},{4,7},{5,4},{6,5},{7,6},{8,11},{9,8},{10,9... | collective-permute-start | bytes 196616 | tf_op jit(solution)/shard_map/ppermute | solution.py:331
  8.2 0.7 copy-start.1
  10.9 16.4 %copy-start.2 = (s32[16]{0:T(128)S(1)}, s32[16]{0:T(128)}, u32[]{:S(2)}) copy-start(s32[16]{0:T(128)} %doc_start.9) | copy-start | bytes 196
  11.3 13.9 %collective-permute-start.3 = (bf16[1040,256]{1,0:T(8,128)(2,1)S(1)}, bf16[1040,256]{1,0:T(8,128)(2,1)S(1)}, u32[]{:S(2)}, u32[]{:S(2)}) collective-permute-start(bf16[1040,256]{1,0:T(8,128)(2,1)S(1)} %get-tuple-element.52), channel_id=1, source_target_pairs={{0,1},{1,2},{2,3},{3,0},{4,5},{5,6},{6,7},{7,4},{8,9},{9,10},{10,1... | collective-permute-start | bytes 1597448 | tf_op jit(solution)/shard_map/ppermute | solution.py:331
  11.7 13.5 %collective-permute-start.4 = (bf16[1040,256]{1,0:T(8,128)(2,1)S(1)}, bf16[1040,256]{1,0:T(8,128)(2,1)S(1)}, u32[]{:S(2)}, u32[]{:S(2)}) collective-permute-start(bf16[1040,256]{1,0:T(8,128)(2,1)S(1)} %get-tuple-element.53), channel_id=1, source_target_pairs={{0,3},{1,0},{2,1},{3,2},{4,7},{5,4},{6,5},{7,6},{8,11},{9,8},{10,9... | collective-permute-start | bytes 1597448 | tf_op jit(solution)/shard_map/ppermute | solution.py:331
  14.6 22.6 %collective-permute-start.7 = (bf16[4,128,256]{2,1,0:T(8,128)(2,1)S(1)}, bf16[4,128,256]{2,1,0:T(8,128)(2,1)S(1)}, u32[]{:S(2)}, u32[]{:S(2)}) collective-permute-start(bf16[4,128,256]{2,1,0:T(8,128)(2,1)S(1)} %get-tuple-element.62.kv), channel_id=1, source_target_pairs={{0,4},{1,5},{2,6},{3,7},{4,8},{5,9},{6,10},{7,11},{8,12},{9,13},{1... | collective-permute-start | bytes 786440 | tf_op jit(solution)/shard_map/ppermute | solution.py:335
  18.0 23.3 %collective-permute-start.6 = (bf16[3,128,256]{2,1,0:T(8,128)(2,1)S(1)}, bf16[3,128,256]{2,1,0:T(8,128)(2,1)S(1)}, u32[]{:S(2)}, u32[]{:S(2)}) collective-permute-start(bf16[3,128,256]{2,1,0:T(8,128)(2,1)S(1)} %get-tuple-element.67), channel_id=1, source_target_pairs={{0,8},{1,9},{2,10},{3,11},{4,12},{5,13},{6,14},{7,15},{8,16},{9,17... | collective-permute-start | bytes 589832 | tf_op jit(solution)/shard_map/ppermute | solution.py:335
  25.2 14.0 %collective-permute-start.5 = (bf16[1040,256]{1,0:T(8,128)(2,1)S(1)}, bf16[1040,256]{1,0:T(8,128)(2,1)S(1)}, u32[]{:S(2)}, u32[]{:S(2)}) collective-permute-start(bf16[1040,256]{1,0:T(8,128)(2,1)S(1)} %get-tuple-element.61), channel_id=1, source_target_pairs={{0,2},{1,3},{2,0},{3,1},{4,6},{5,7},{6,4},{7,5},{8,10},{9,11},{10,... | collective-permute-start | bytes 1597448 | tf_op jit(solution)/shard_map/ppermute | solution.py:331
  40.4 25.7 %collective-permute-start.11 = (bf16[4,128,256]{2,1,0:T(8,128)(2,1)S(1)}, bf16[4,128,256]{2,1,0:T(8,128)(2,1)S(1)}, u32[]{:S(2)}, u32[]{:S(2)}) collective-permute-start(bf16[4,128,256]{2,1,0:T(8,128)(2,1)S(1)} %get-tuple-element.79), channel_id=1, source_target_pairs={{0,252},{1,253},{2,254},{3,255},{4,0},{5,1},{6,2},{7,3},{8,4},{9,5... | collective-permute-start | bytes 786440 | tf_op jit(solution)/shard_map/ppermute | solution.py:335
  42.2 23.9 %collective-permute-start.12 = (bf16[3,128,256]{2,1,0:T(8,128)(2,1)S(1)}, bf16[3,128,256]{2,1,0:T(8,128)(2,1)S(1)}, u32[]{:S(2)}, u32[]{:S(2)}) collective-permute-start(bf16[3,128,256]{2,1,0:T(8,128)(2,1)S(1)} %get-tuple-element.80), channel_id=1, source_target_pairs={{0,248},{1,249},{2,250},{3,251},{4,252},{5,253},{6,254},{7,255},{8... | collective-permute-start | bytes 589832 | tf_op jit(solution)/shard_map/ppermute | solution.py:335
  47.9 20.3 %collective-permute-start.8 = (bf16[128,1024]{1,0:T(8,128)(2,1)S(1)}, bf16[128,1024]{1,0:T(8,128)(2,1)S(1)}, u32[]{:S(2)}, u32[]{:S(2)}) collective-permute-start(bf16[128,1024]{1,0:T(8,128)(2,1)S(1)} %get-tuple-element.75), channel_id=1, source_target_pairs={{0,3},{1,0},{2,1},{3,2},{4,7},{5,4},{6,5},{7,6},{8,11},{9,8},{10,9... | collective-permute-start | bytes 786440 | tf_op jit(solution)/shard_map/ppermute | solution.py:331
  49.1 20.4 %collective-permute-start.9 = (bf16[128,1024]{1,0:T(8,128)(2,1)S(1)}, bf16[128,1024]{1,0:T(8,128)(2,1)S(1)}, u32[]{:S(2)}, u32[]{:S(2)}) collective-permute-start(bf16[128,1024]{1,0:T(8,128)(2,1)S(1)} %get-tuple-element.76), channel_id=1, source_target_pairs={{0,2},{1,3},{2,0},{3,1},{4,6},{5,7},{6,4},{7,5},{8,10},{9,11},{10,... | collective-permute-start | bytes 786440 | tf_op jit(solution)/shard_map/ppermute | solution.py:331
  49.1 20.4 %collective-permute-start.10 = (bf16[128,1024]{1,0:T(8,128)(2,1)S(1)}, bf16[128,1024]{1,0:T(8,128)(2,1)S(1)}, u32[]{:S(2)}, u32[]{:S(2)}) collective-permute-start(bf16[128,1024]{1,0:T(8,128)(2,1)S(1)} %get-tuple-element.77), channel_id=1, source_target_pairs={{0,1},{1,2},{2,3},{3,0},{4,5},{5,6},{6,7},{7,4},{8,9},{9,10},{10,1... | collective-permute-start | bytes 786440 | tf_op jit(solution)/shard_map/ppermute | solution.py:331
  66.2 4.4 %collective-permute-start.13 = (bf16[128,256]{1,0:T(8,128)(2,1)S(1)}, bf16[128,256]{1,0:T(8,128)(2,1)S(1)}, u32[]{:S(2)}, u32[]{:S(2)}) collective-permute-start(bf16[128,256]{1,0:T(8,128)(2,1)S(1)} %get-tuple-element.82), channel_id=1, source_target_pairs={{0,3},{1,0},{2,1},{3,2},{4,7},{5,4},{6,5},{7,6},{8,11},{9,8},{10,9... | collective-permute-start | bytes 196616 | tf_op jit(solution)/shard_map/ppermute | solution.py:331
  66.3 6.0 %collective-permute-start.14 = (bf16[128,256]{1,0:T(8,128)(2,1)S(1)}, bf16[128,256]{1,0:T(8,128)(2,1)S(1)}, u32[]{:S(2)}, u32[]{:S(2)}) collective-permute-start(bf16[128,256]{1,0:T(8,128)(2,1)S(1)} %get-tuple-element.83), channel_id=1, source_target_pairs={{0,2},{1,3},{2,0},{3,1},{4,6},{5,7},{6,4},{7,5},{8,10},{9,11},{10,... | collective-permute-start | bytes 196616 | tf_op jit(solution)/shard_map/ppermute | solution.py:331
  68.3 5.5 %collective-permute-start.15 = (bf16[128,256]{1,0:T(8,128)(2,1)S(1)}, bf16[128,256]{1,0:T(8,128)(2,1)S(1)}, u32[]{:S(2)}, u32[]{:S(2)}) collective-permute-start(bf16[128,256]{1,0:T(8,128)(2,1)S(1)} %get-tuple-element.84), channel_id=1, source_target_pairs={{0,1},{1,2},{2,3},{3,0},{4,5},{5,6},{6,7},{7,4},{8,9},{9,10},{10,1... | collective-permute-start | bytes 196616 | tf_op jit(solution)/shard_map/ppermute | solution.py:331

commit v3 on v2

--- a/solution.py
+++ b/solution.py
@@ -191,18 +191,19 @@
 
             return carry
 
-        if back == 1:
-            whole = first_key >= start
+        if back > 0:
+            count = ROW - 1 if back == 2 else ROW
+            whole = first_key + ROW - count >= start
 
             @pl.when(whole)
-            def _(work=work):
-                work(0, ROW)
+            def _(work=work, count=count):
+                work(0, count)
 
             @pl.when(jnp.logical_not(whole))
-            def _(turn=turn):
-                lax.fori_loop(1, ROW, turn, 0)
+            def _(turn=turn, count=count):
+                lax.fori_loop(1, count, turn, 0)
         else:
-            lax.fori_loop(0, ROW - 1 if back == 2 else ROW, turn, 0)
+            lax.fori_loop(0, ROW, turn, 0)
 
 
 def begin_own(doc_start, piece0, piece1, piece3, kv, dkv, dq):

time: 75.4 us -> 75.5 us (level)
  the two profiles are of different devices: /device:TPU:38 before, /device:TPU:36 now
where the time goes in v3:
time: 75.5 us; the launch traced here: 75.1 us
  starting transfers between devices  26.9 us (36%)
  waiting for transfers between devices  26.9 us (36%)
  Pallas kernels  19.7 us (26%)
  between operations  0.96 us (1%)
    ppermute x4, waiting for transfers between devices, along_rows(): lax.ppermute(value, AXES, [(b, (b + by) % total) for b in range(total)])  21.5 us
    ppermute x12, starting transfers between devices, along_row(): return lax.ppermute(value, AXES, pairs)  18 us
    ppermute x4, starting transfers between devices, along_rows(): lax.ppermute(value, AXES, [(b, (b + by) % total) for b in range(total)])  8.89 us
    ppermute x12, waiting for transfers between devices, along_row(): return lax.ppermute(value, AXES, pairs)  5.42 us
    pallas_call x1, Pallas kernels, per_device(): kernel(begin_own, 'begin_own', [SMEM] + [VMEM] * 4, [(kv_shape, F32), dq_...  3.24 us
    pallas_call x1, Pallas kernels, per_device(): kernel(finish_own, 'finish_own', [SMEM] + [VMEM] * 5, [(kv_shape, F32)] +...  3.07 us
    pallas_call x1, Pallas kernels, per_device(): kernel(begin_one, 'begin_one', [SMEM] + [VMEM] * 5, [(kv_shape, F32), dq_...  3.07 us
    pallas_call x1, Pallas kernels, per_device(): kernel(functools.partial(pack, (1, 3)), 'pack_near', [HBM] * 4, [piece_sh...  1.95 us
  transfers between devices with their start and end apart: 16, of which 7 were waited for; matrix products, arithmetic and copies ran while one was open for 0% of the time, Pallas kernels for 23%

profile of v3, /device:TPU:36, one launch (start us, length us, event | category | flops | bytes accessed | tf_op | source)
XLA Modules:
  0.0 75.1 jit_solution(14508429041455796482)
XLA Ops:
  0.6 1.6 %pack_kv.1 = (bf16[128,256]{1,0:T(8,128)(2,1)}, bf16[128,256]{1,0:T(8,128)(2,1)}, bf16[128,256]{1,0:T(8,128)(2,1)}, bf16[128,256]{1,0:T(8,128)(2,1)}) custom-call(bf16[128,512]{1,0:T(8,128)(2,1)} %keys.1, bf16[128,512]{1,0:T(8,128)(2,1)} %values.1), custom_call_target="tpu_custom_call" | custom-call | tf_op jit(solution)/shard_map/pack_kv/pallas_call | solution.py:352
  2.3 0.0 copy-start
  2.3 1.7 %collective-permute-start = (bf16[128,256]{1,0:T(8,128)(2,1)}, bf16[128,256]{1,0:T(8,128)(2,1)S(1)}, u32[]{:S(2)}, u32[]{:S(2)}) collective-permute-start(bf16[128,256]{1,0:T(8,128)(2,1)} %get-tuple-element.46), channel_id=1, source_target_pairs={{0,1},{1,2},{2,3},{3,0},{4,5},{5,6},{6,7},{7,4},{8,9},{9,10},{10,1... | collective-permute-start | bytes 196616 | tf_op jit(solution)/shard_map/ppermute | solution.py:332
  3.9 2.9 %collective-permute-start.1 = (bf16[128,256]{1,0:T(8,128)(2,1)}, bf16[128,256]{1,0:T(8,128)(2,1)S(1)}, u32[]{:S(2)}, u32[]{:S(2)}) collective-permute-start(bf16[128,256]{1,0:T(8,128)(2,1)} %get-tuple-element.47), channel_id=1, source_target_pairs={{0,2},{1,3},{2,0},{3,1},{4,6},{5,7},{6,4},{7,5},{8,10},{9,11},{10,... | collective-permute-start | bytes 196616 | tf_op jit(solution)/shard_map/ppermute | solution.py:332
  6.8 1.3 %collective-permute-start.2 = (bf16[128,256]{1,0:T(8,128)(2,1)}, bf16[128,256]{1,0:T(8,128)(2,1)S(1)}, u32[]{:S(2)}, u32[]{:S(2)}) collective-permute-start(bf16[128,256]{1,0:T(8,128)(2,1)} %get-tuple-element.48), channel_id=1, source_target_pairs={{0,3},{1,0},{2,1},{3,2},{4,7},{5,4},{6,5},{7,6},{8,11},{9,8},{10,9... | collective-permute-start | bytes 196616 | tf_op jit(solution)/shard_map/ppermute | solution.py:332
  8.2 0.7 copy-done.1
  8.9 2.0 %pack_near.1 = (bf16[1040,256]{1,0:T(8,128)(2,1)S(1)}, bf16[1040,256]{1,0:T(8,128)(2,1)S(1)}) custom-call(bf16[128,4096]{1,0:T(8,128)(2,1)} %queries.3, bf16[128,4096]{1,0:T(8,128)(2,1)} %outputs.3, bf16[128,4096]{1,0:T(8,128)(2,1)} %grads.1, bf16[32,128]{1,0:T(8,128)(2,1)S(1)} %bitcast.1), custom_call_target="tpu_custom_call" | custom-call | tf_op jit(solution)/shard_map/pack_near/pallas_call | solution.py:357
  10.9 0.0 copy-start.2
  10.9 0.0 collective-permute-done.piece1
  10.9 0.0 collective-permute-done.1.piece2
  10.9 0.4 collective-permute-done.2.piece3
  11.3 0.3 collective-permute-start.3
  11.7 2.9 %collective-permute-start.4 = (bf16[1040,256]{1,0:T(8,128)(2,1)S(1)}, bf16[1040,256]{1,0:T(8,128)(2,1)S(1)}, u32[]{:S(2)}, u32[]{:S(2)}) collective-permute-start(bf16[1040,256]{1,0:T(8,128)(2,1)S(1)} %get-tuple-element.53), channel_id=1, source_target_pairs={{0,3},{1,0},{2,1},{3,2},{4,7},{5,4},{6,5},{7,6},{8,11},{9,8},{10,9... | collective-permute-start | bytes 1597448 | tf_op jit(solution)/shard_map/ppermute | solution.py:332
  14.6 0.0 copy-done
  14.6 3.3 %collective-permute-start.7 = (bf16[4,128,256]{2,1,0:T(8,128)(2,1)S(1)}, bf16[4,128,256]{2,1,0:T(8,128)(2,1)S(1)}, u32[]{:S(2)}, u32[]{:S(2)}) collective-permute-start(bf16[4,128,256]{2,1,0:T(8,128)(2,1)S(1)} %get-tuple-element.62.kv), channel_id=1, source_target_pairs={{0,4},{1,5},{2,6},{3,7},{4,8},{5,9},{6,10},{7,11},{8,12},{9,13},{1... | collective-permute-start | bytes 786440 | tf_op jit(solution)/shard_map/ppermute | solution.py:336
  18.0 4.5 %collective-permute-start.6 = (bf16[3,128,256]{2,1,0:T(8,128)(2,1)S(1)}, bf16[3,128,256]{2,1,0:T(8,128)(2,1)S(1)}, u32[]{:S(2)}, u32[]{:S(2)}) collective-permute-start(bf16[3,128,256]{2,1,0:T(8,128)(2,1)S(1)} %get-tuple-element.67), channel_id=1, source_target_pairs={{0,8},{1,9},{2,10},{3,11},{4,12},{5,13},{6,14},{7,15},{8,16},{9,17... | collective-permute-start | bytes 589832 | tf_op jit(solution)/shard_map/ppermute | solution.py:336
  22.5 2.0 %pack_rest.1 = (bf16[1040,256]{1,0:T(8,128)(2,1)S(1)}, bf16[1040,256]{1,0:T(8,128)(2,1)S(1)}) custom-call(bf16[128,4096]{1,0:T(8,128)(2,1)} %queries.3, bf16[128,4096]{1,0:T(8,128)(2,1)} %outputs.3, bf16[128,4096]{1,0:T(8,128)(2,1)} %grads.1, bf16[32,128]{1,0:T(8,128)(2,1)S(1)} %bitcast.2), custom_call_target="tpu_custom_call" | custom-call | tf_op jit(solution)/shard_map/pack_rest/pallas_call | solution.py:374
  24.4 0.8 %collective-permute-done.3.piece1 = bf16[1040,256]{1,0:T(8,128)(2,1)S(1)} collective-permute-done((bf16[1040,256]{1,0:T(8,128)(2,1)S(1)}, bf16[1040,256]{1,0:T(8,128)(2,1)S(1)}, u32[]{:S(2)}, u32[]{:S(2)}) %collective-permute-start.3) | collective-permute-done | bytes 532512 | tf_op jit(solution)/shard_map/ppermute | solution.py:332
  25.2 0.0 collective-permute-done.4.piece3
  25.2 2.1 %collective-permute-start.5 = (bf16[1040,256]{1,0:T(8,128)(2,1)S(1)}, bf16[1040,256]{1,0:T(8,128)(2,1)S(1)}, u32[]{:S(2)}, u32[]{:S(2)}) collective-permute-start(bf16[1040,256]{1,0:T(8,128)(2,1)S(1)} %get-tuple-element.61), channel_id=1, source_target_pairs={{0,2},{1,3},{2,0},{3,1},{4,6},{5,7},{6,4},{7,5},{8,10},{9,11},{10,... | collective-permute-start | bytes 1597448 | tf_op jit(solution)/shard_map/ppermute | solution.py:332
  27.3 0.0 copy-done.2
  27.3 3.2 %begin_own.1 = (f32[4,128,256]{2,1,0:T(8,128)S(1)}, f32[4,128,1024]{2,1,0:T(8,128)S(1)}) custom-call(s32[16]{0:T(128)S(1)} %copy-done.2, bf16[1040,256]{1,0:T(8,128)(2,1)S(1)} %get-tuple-element.63.piece0, bf16[1040,256]{1,0:T(8,128)(2,1)S(1)} %collective-permute-done.3.piece1, bf16[1040,256]{1,0:T(8,128)(2,1)S(1)} %collective-permute-done.4.piece3, ...), custom_call_target="tpu_custom_call" | custom-call | flops 20000000000 | bytes 20000000000 | tf_op jit(solution)/shard_map/begin_own/pallas_call | solution.py:385
  30.5 6.1 %collective-permute-done.7.kv = bf16[4,128,256]{2,1,0:T(8,128)(2,1)S(1)} collective-permute-done((bf16[4,128,256]{2,1,0:T(8,128)(2,1)S(1)}, bf16[4,128,256]{2,1,0:T(8,128)(2,1)S(1)}, u32[]{:S(2)}, u32[]{:S(2)}) %collective-permute-start.7) | collective-permute-done | bytes 262176 | tf_op jit(solution)/shard_map/ppermute | solution.py:336
  36.6 3.1 %begin_one.1 = (f32[4,128,256]{2,1,0:T(8,128)S(1)}, f32[4,128,1024]{2,1,0:T(8,128)S(1)}) custom-call(s32[16]{0:T(128)S(1)} %copy-done.2, bf16[1040,256]{1,0:T(8,128)(2,1)S(1)} %get-tuple-element.63.piece0, bf16[1040,256]{1,0:T(8,128)(2,1)S(1)} %collective-permute-done.3.piece1, bf16[1040,256]{1,0:T(8,128)(2,1)S(1)} %collective-permute-done.4.piece3, ...), custom_call_target="tpu_custom_call" | custom-call | flops 20000000000 | bytes 20000000000 | tf_op jit(solution)/shard_map/begin_one/pallas_call | solution.py:388
  39.7 0.0 collective-permute-done.5.piece2
  39.7 1.7 %finish_one.1 = (bf16[4,128,256]{2,1,0:T(8,128)(2,1)S(1)}, f32[1,128,1024]{2,1,0:T(8,128)S(1)}) custom-call(s32[16]{0:T(128)S(1)} %copy-done.2, bf16[1040,256]{1,0:T(8,128)(2,1)S(1)} %collective-permute-done.5.piece2, bf16[4,128,256]{2,1,0:T(8,128)(2,1)S(1)} %collective-permute-done.7.kv, f32[4,128,256]{2,1,0:T(8,128)S(1)} %get-tuple-element.70.one_in), custom_call_target="tpu_custom_call" | custom-call | flops 20000000000 | bytes 20000000000 | tf_op jit(solution)/shard_map/finish_one/pallas_call | solution.py:392
  41.4 0.1 collective-permute-start.11
  41.5 0.0 collective-permute-done.6.kv
  41.5 1.1 %all_two.1 = (bf16[3,128,256]{2,1,0:T(8,128)(2,1)S(1)}, f32[4,128,1024]{2,1,0:T(8,128)S(1)}, f32[1,128,1024]{2,1,0:T(8,128)S(1)}) custom-call(s32[16]{0:T(128)S(1)} %copy-done.2, bf16[1040,256]{1,0:T(8,128)(2,1)S(1)} %get-tuple-element.63.piece0, bf16[1040,256]{1,0:T(8,128)(2,1)S(1)} %collective-permute-done.3.piece1, ...), custom_call_target="tpu_custom_call" | custom-call | flops 20000000000 | bytes 20000000000 | tf_op jit(solution)/shard_map/all_two/pallas_call | solution.py:400
  42.6 0.9 %collective-permute-start.12 = (bf16[3,128,256]{2,1,0:T(8,128)(2,1)S(1)}, bf16[3,128,256]{2,1,0:T(8,128)(2,1)S(1)}, u32[]{:S(2)}, u32[]{:S(2)}) collective-permute-start(bf16[3,128,256]{2,1,0:T(8,128)(2,1)S(1)} %get-tuple-element.80), channel_id=1, source_target_pairs={{0,248},{1,249},{2,250},{3,251},{4,252},{5,253},{6,254},{7,255},{8... | collective-permute-start | bytes 589832 | tf_op jit(solution)/shard_map/ppermute | solution.py:336
  43.6 3.1 %finish_own.1 = (f32[4,128,256]{2,1,0:T(8,128)S(1)}, bf16[128,1024]{1,0:T(8,128)(2,1)S(1)}, bf16[128,1024]{1,0:T(8,128)(2,1)S(1)}, bf16[128,1024]{1,0:T(8,128)(2,1)S(1)}, bf16[128,1024]{1,0:T(8,128)(2,1)S(1)}) custom-call(s32[16]{0:T(128)S(1)} %copy-done.2, bf16[1040,256]{1,0:T(8,128)(2,1)S(1)} %collective-permute-done.5.piece2, ...), custom_call_target="tpu_custom_call" | custom-call | tf_op jit(solution)/shard_map/finish_own/pallas_call | solution.py:410
  46.7 1.9 %collective-permute-start.8 = (bf16[128,1024]{1,0:T(8,128)(2,1)S(1)}, bf16[128,1024]{1,0:T(8,128)(2,1)S(1)}, u32[]{:S(2)}, u32[]{:S(2)}) collective-permute-start(bf16[128,1024]{1,0:T(8,128)(2,1)S(1)} %get-tuple-element.75), channel_id=1, source_target_pairs={{0,3},{1,0},{2,1},{3,2},{4,7},{5,4},{6,5},{7,6},{8,11},{9,8},{10,9... | collective-permute-start | bytes 786440 | tf_op jit(solution)/shard_map/ppermute | solution.py:332
  48.5 0.0 collective-permute-start.9
  48.5 1.0 %collective-permute-start.10 = (bf16[128,1024]{1,0:T(8,128)(2,1)S(1)}, bf16[128,1024]{1,0:T(8,128)(2,1)S(1)}, u32[]{:S(2)}, u32[]{:S(2)}) collective-permute-start(bf16[128,1024]{1,0:T(8,128)(2,1)S(1)} %get-tuple-element.77), channel_id=1, source_target_pairs={{0,1},{1,2},{2,3},{3,0},{4,5},{5,6},{6,7},{7,4},{8,9},{9,10},{10,1... | collective-permute-start | bytes 786440 | tf_op jit(solution)/shard_map/ppermute | solution.py:332
  49.5 15.4 %collective-permute-done.12.two = bf16[3,128,256]{2,1,0:T(8,128)(2,1)S(1)} collective-permute-done((bf16[3,128,256]{2,1,0:T(8,128)(2,1)S(1)}, bf16[3,128,256]{2,1,0:T(8,128)(2,1)S(1)}, u32[]{:S(2)}, u32[]{:S(2)}) %collective-permute-start.12) | collective-permute-done | bytes 196640 | tf_op jit(solution)/shard_map/ppermute | solution.py:336
  64.9 0.0 collective-permute-done.11.one
  64.9 0.1 add_up.1
  65.0 3.0 %collective-permute-start.13 = (bf16[128,256]{1,0:T(8,128)(2,1)S(1)}, bf16[128,256]{1,0:T(8,128)(2,1)S(1)}, u32[]{:S(2)}, u32[]{:S(2)}) collective-permute-start(bf16[128,256]{1,0:T(8,128)(2,1)S(1)} %get-tuple-element.82), channel_id=1, source_target_pairs={{0,3},{1,0},{2,1},{3,2},{4,7},{5,4},{6,5},{7,6},{8,11},{9,8},{10,9... | collective-permute-start | bytes 196616 | tf_op jit(solution)/shard_map/ppermute | solution.py:332
  68.0 0.0 collective-permute-start.14
  68.0 0.0 collective-permute-done.8.piece1
  68.0 1.0 %collective-permute-start.15 = (bf16[128,256]{1,0:T(8,128)(2,1)S(1)}, bf16[128,256]{1,0:T(8,128)(2,1)S(1)}, u32[]{:S(2)}, u32[]{:S(2)}) collective-permute-start(bf16[128,256]{1,0:T(8,128)(2,1)S(1)} %get-tuple-element.84), channel_id=1, source_target_pairs={{0,1},{1,2},{2,3},{3,0},{4,5},{5,6},{6,7},{7,4},{8,9},{9,10},{10,1... | collective-permute-start | bytes 196616 | tf_op jit(solution)/shard_map/ppermute | solution.py:332
  68.9 0.0 collective-permute-done.9.piece2
  68.9 0.0 collective-permute-done.10.piece3
  69.0 1.0 %join_queries.1 = bf16[128,4096]{1,0:T(8,128)(2,1)} custom-call(bf16[128,1024]{1,0:T(8,128)(2,1)S(1)} %get-tuple-element.74.piece0, bf16[128,1024]{1,0:T(8,128)(2,1)S(1)} %collective-permute-done.8.piece1, bf16[128,1024]{1,0:T(8,128)(2,1)S(1)} %collective-permute-done.9.piece2, bf16[128,1024]{1,0:T(8,128)(2,1)S(1)} %collective-permute-done.10.piece3), custom_call_target="tpu_custom_call" | custom-call | tf_op jit(solution)/shard_map/join_queries/pallas_call | solution.py:419
  70.0 0.5 collective-permute-done.13.piece1
  70.5 3.4 %collective-permute-done.14.piece2 = bf16[128,256]{1,0:T(8,128)(2,1)S(1)} collective-permute-done((bf16[128,256]{1,0:T(8,128)(2,1)S(1)}, bf16[128,256]{1,0:T(8,128)(2,1)S(1)}, u32[]{:S(2)}, u32[]{:S(2)}) %collective-permute-start.14) | collective-permute-done | bytes 65568 | tf_op jit(solution)/shard_map/ppermute | solution.py:332
  73.9 0.3 collective-permute-done.15.piece3
  74.2 0.8 %join_kv.1 = (bf16[128,512]{1,0:T(8,128)(2,1)}, bf16[128,512]{1,0:T(8,128)(2,1)}) custom-call(bf16[128,256]{1,0:T(8,128)(2,1)S(1)} %get-tuple-element.81.piece0, bf16[128,256]{1,0:T(8,128)(2,1)S(1)} %collective-permute-done.13.piece1, bf16[128,256]{1,0:T(8,128)(2,1)S(1)} %collective-permute-done.14.piece2, bf16[128,256]{1,0:T(8,128)(2,1)S(1)} %collective-permute-done.15.piece3), custom_call_target="tpu_custom_call" | custom-call | tf_op jit(solution)/shard_map/join_kv/pallas_call | solution.py:433
  (2 shorter events, 0.0 us)
Async XLA Ops:
  2.3 12.3 %copy-start = (bf16[128,256]{1,0:T(8,128)(2,1)S(1)}, bf16[128,256]{1,0:T(8,128)(2,1)}, u32[]{:S(2)}) copy-start(bf16[128,256]{1,0:T(8,128)(2,1)} %get-tuple-element.54.piece0) | copy-start | bytes 196612
  2.3 8.6 %collective-permute-start = (bf16[128,256]{1,0:T(8,128)(2,1)}, bf16[128,256]{1,0:T(8,128)(2,1)S(1)}, u32[]{:S(2)}, u32[]{:S(2)}) collective-permute-start(bf16[128,256]{1,0:T(8,128)(2,1)} %get-tuple-element.46), channel_id=1, source_target_pairs={{0,1},{1,2},{2,3},{3,0},{4,5},{5,6},{6,7},{7,4},{8,9},{9,10},{10,1... | collective-permute-start | bytes 196616 | tf_op jit(solution)/shard_map/ppermute | solution.py:332
  3.9 6.9 %collective-permute-start.1 = (bf16[128,256]{1,0:T(8,128)(2,1)}, bf16[128,256]{1,0:T(8,128)(2,1)S(1)}, u32[]{:S(2)}, u32[]{:S(2)}) collective-permute-start(bf16[128,256]{1,0:T(8,128)(2,1)} %get-tuple-element.47), channel_id=1, source_target_pairs={{0,2},{1,3},{2,0},{3,1},{4,6},{5,7},{6,4},{7,5},{8,10},{9,11},{10,... | collective-permute-start | bytes 196616 | tf_op jit(solution)/shard_map/ppermute | solution.py:332
  6.8 4.5 %collective-permute-start.2 = (bf16[128,256]{1,0:T(8,128)(2,1)}, bf16[128,256]{1,0:T(8,128)(2,1)S(1)}, u32[]{:S(2)}, u32[]{:S(2)}) collective-permute-start(bf16[128,256]{1,0:T(8,128)(2,1)} %get-tuple-element.48), channel_id=1, source_target_pairs={{0,3},{1,0},{2,1},{3,2},{4,7},{5,4},{6,5},{7,6},{8,11},{9,8},{10,9... | collective-permute-start | bytes 196616 | tf_op jit(solution)/shard_map/ppermute | solution.py:332
  8.2 0.7 copy-start.1
  10.9 16.4 %copy-start.2 = (s32[16]{0:T(128)S(1)}, s32[16]{0:T(128)}, u32[]{:S(2)}) copy-start(s32[16]{0:T(128)} %doc_start.9) | copy-start | bytes 196
  11.3 13.9 %collective-permute-start.3 = (bf16[1040,256]{1,0:T(8,128)(2,1)S(1)}, bf16[1040,256]{1,0:T(8,128)(2,1)S(1)}, u32[]{:S(2)}, u32[]{:S(2)}) collective-permute-start(bf16[1040,256]{1,0:T(8,128)(2,1)S(1)} %get-tuple-element.52), channel_id=1, source_target_pairs={{0,1},{1,2},{2,3},{3,0},{4,5},{5,6},{6,7},{7,4},{8,9},{9,10},{10,1... | collective-permute-start | bytes 1597448 | tf_op jit(solution)/shard_map/ppermute | solution.py:332
  11.7 13.5 %collective-permute-start.4 = (bf16[1040,256]{1,0:T(8,128)(2,1)S(1)}, bf16[1040,256]{1,0:T(8,128)(2,1)S(1)}, u32[]{:S(2)}, u32[]{:S(2)}) collective-permute-start(bf16[1040,256]{1,0:T(8,128)(2,1)S(1)} %get-tuple-element.53), channel_id=1, source_target_pairs={{0,3},{1,0},{2,1},{3,2},{4,7},{5,4},{6,5},{7,6},{8,11},{9,8},{10,9... | collective-permute-start | bytes 1597448 | tf_op jit(solution)/shard_map/ppermute | solution.py:332
  14.6 22.0 %collective-permute-start.7 = (bf16[4,128,256]{2,1,0:T(8,128)(2,1)S(1)}, bf16[4,128,256]{2,1,0:T(8,128)(2,1)S(1)}, u32[]{:S(2)}, u32[]{:S(2)}) collective-permute-start(bf16[4,128,256]{2,1,0:T(8,128)(2,1)S(1)} %get-tuple-element.62.kv), channel_id=1, source_target_pairs={{0,4},{1,5},{2,6},{3,7},{4,8},{5,9},{6,10},{7,11},{8,12},{9,13},{1... | collective-permute-start | bytes 786440 | tf_op jit(solution)/shard_map/ppermute | solution.py:336
  18.0 23.6 %collective-permute-start.6 = (bf16[3,128,256]{2,1,0:T(8,128)(2,1)S(1)}, bf16[3,128,256]{2,1,0:T(8,128)(2,1)S(1)}, u32[]{:S(2)}, u32[]{:S(2)}) collective-permute-start(bf16[3,128,256]{2,1,0:T(8,128)(2,1)S(1)} %get-tuple-element.67), channel_id=1, source_target_pairs={{0,8},{1,9},{2,10},{3,11},{4,12},{5,13},{6,14},{7,15},{8,16},{9,17... | collective-permute-start | bytes 589832 | tf_op jit(solution)/shard_map/ppermute | solution.py:336
  25.2 14.5 %collective-permute-start.5 = (bf16[1040,256]{1,0:T(8,128)(2,1)S(1)}, bf16[1040,256]{1,0:T(8,128)(2,1)S(1)}, u32[]{:S(2)}, u32[]{:S(2)}) collective-permute-start(bf16[1040,256]{1,0:T(8,128)(2,1)S(1)} %get-tuple-element.61), channel_id=1, source_target_pairs={{0,2},{1,3},{2,0},{3,1},{4,6},{5,7},{6,4},{7,5},{8,10},{9,11},{10,... | collective-permute-start | bytes 1597448 | tf_op jit(solution)/shard_map/ppermute | solution.py:332
  41.4 23.5 %collective-permute-start.11 = (bf16[4,128,256]{2,1,0:T(8,128)(2,1)S(1)}, bf16[4,128,256]{2,1,0:T(8,128)(2,1)S(1)}, u32[]{:S(2)}, u32[]{:S(2)}) collective-permute-start(bf16[4,128,256]{2,1,0:T(8,128)(2,1)S(1)} %get-tuple-element.79), channel_id=1, source_target_pairs={{0,252},{1,253},{2,254},{3,255},{4,0},{5,1},{6,2},{7,3},{8,4},{9,5... | collective-permute-start | bytes 786440 | tf_op jit(solution)/shard_map/ppermute | solution.py:336
  42.6 22.3 %collective-permute-start.12 = (bf16[3,128,256]{2,1,0:T(8,128)(2,1)S(1)}, bf16[3,128,256]{2,1,0:T(8,128)(2,1)S(1)}, u32[]{:S(2)}, u32[]{:S(2)}) collective-permute-start(bf16[3,128,256]{2,1,0:T(8,128)(2,1)S(1)} %get-tuple-element.80), channel_id=1, source_target_pairs={{0,248},{1,249},{2,250},{3,251},{4,252},{5,253},{6,254},{7,255},{8... | collective-permute-start | bytes 589832 | tf_op jit(solution)/shard_map/ppermute | solution.py:336
  46.7 21.3 %collective-permute-start.8 = (bf16[128,1024]{1,0:T(8,128)(2,1)S(1)}, bf16[128,1024]{1,0:T(8,128)(2,1)S(1)}, u32[]{:S(2)}, u32[]{:S(2)}) collective-permute-start(bf16[128,1024]{1,0:T(8,128)(2,1)S(1)} %get-tuple-element.75), channel_id=1, source_target_pairs={{0,3},{1,0},{2,1},{3,2},{4,7},{5,4},{6,5},{7,6},{8,11},{9,8},{10,9... | collective-permute-start | bytes 786440 | tf_op jit(solution)/shard_map/ppermute | solution.py:332
  48.5 20.4 %collective-permute-start.9 = (bf16[128,1024]{1,0:T(8,128)(2,1)S(1)}, bf16[128,1024]{1,0:T(8,128)(2,1)S(1)}, u32[]{:S(2)}, u32[]{:S(2)}) collective-permute-start(bf16[128,1024]{1,0:T(8,128)(2,1)S(1)} %get-tuple-element.76), channel_id=1, source_target_pairs={{0,2},{1,3},{2,0},{3,1},{4,6},{5,7},{6,4},{7,5},{8,10},{9,11},{10,... | collective-permute-start | bytes 786440 | tf_op jit(solution)/shard_map/ppermute | solution.py:332
  48.5 20.4 %collective-permute-start.10 = (bf16[128,1024]{1,0:T(8,128)(2,1)S(1)}, bf16[128,1024]{1,0:T(8,128)(2,1)S(1)}, u32[]{:S(2)}, u32[]{:S(2)}) collective-permute-start(bf16[128,1024]{1,0:T(8,128)(2,1)S(1)} %get-tuple-element.77), channel_id=1, source_target_pairs={{0,1},{1,2},{2,3},{3,0},{4,5},{5,6},{6,7},{7,4},{8,9},{9,10},{10,1... | collective-permute-start | bytes 786440 | tf_op jit(solution)/shard_map/ppermute | solution.py:332
  65.0 5.5 %collective-permute-start.13 = (bf16[128,256]{1,0:T(8,128)(2,1)S(1)}, bf16[128,256]{1,0:T(8,128)(2,1)S(1)}, u32[]{:S(2)}, u32[]{:S(2)}) collective-permute-start(bf16[128,256]{1,0:T(8,128)(2,1)S(1)} %get-tuple-element.82), channel_id=1, source_target_pairs={{0,3},{1,0},{2,1},{3,2},{4,7},{5,4},{6,5},{7,6},{8,11},{9,8},{10,9... | collective-permute-start | bytes 196616 | tf_op jit(solution)/shard_map/ppermute | solution.py:332
  68.0 5.9 %collective-permute-start.14 = (bf16[128,256]{1,0:T(8,128)(2,1)S(1)}, bf16[128,256]{1,0:T(8,128)(2,1)S(1)}, u32[]{:S(2)}, u32[]{:S(2)}) collective-permute-start(bf16[128,256]{1,0:T(8,128)(2,1)S(1)} %get-tuple-element.83), channel_id=1, source_target_pairs={{0,2},{1,3},{2,0},{3,1},{4,6},{5,7},{6,4},{7,5},{8,10},{9,11},{10,... | collective-permute-start | bytes 196616 | tf_op jit(solution)/shard_map/ppermute | solution.py:332
  68.0 6.2 %collective-permute-start.15 = (bf16[128,256]{1,0:T(8,128)(2,1)S(1)}, bf16[128,256]{1,0:T(8,128)(2,1)S(1)}, u32[]{:S(2)}, u32[]{:S(2)}) collective-permute-start(bf16[128,256]{1,0:T(8,128)(2,1)S(1)} %get-tuple-element.84), channel_id=1, source_target_pairs={{0,1},{1,2},{2,3},{3,0},{4,5},{5,6},{6,7},{7,4},{8,9},{9,10},{10,1... | collective-permute-start | bytes 196616 | tf_op jit(solution)/shard_map/ppermute | solution.py:332
